TPU v7x, 128 devices: a whole 4x4x4 slice. The times are simulated.
128 devices in a mesh: src: 8 (over x, core), tgt: 16 (over y, z).
Axes of the slice: x: 4, y: 4, z: 4, core: 2. Of those that a mesh axis runs over, the one named last changes fastest.
Arguments:
- omega: bfloat16 [524288, 128], P(('src', 'tgt')), may hold values from -6 to 6
- owners: int32 [524288, 1], P(('src', 'tgt')), may hold values from 0 to 127; in each aligned block of 4096 rows (0 to 4095, 4096 to 8191, ...) at most 64 rows name the same one
- columns: int32 [524288], P(('src', 'tgt')), may hold values from 0 to 24575
- impedance: float32 [24576], P('tgt'), may hold values from 0.5 to 2
- level_maps: bfloat16 [8, 4, 128, 128], P('src'), may hold values from -0.5 to 0.5
Outputs:
- bases: float32 [8, 24576, 128], P('src', 'tgt')
Inputs may be any that keep to these rules, and one draw needn't show every extreme that they name: `owners`: among the 4096 sampled columns of one device no owner is named more than 64 times, a bound that some block reaches.
All inputs are finite; a program needn't handle non-finite values.
Results may differ from a plain program's by a relative error of at most 0.0035.
Values may be sent and summed in bfloat16 or wider, within the bound.
A program may use at most 128 MiB of HBM per device.

v0:
```python
import functools
import math

import jax
import jax.numpy as jnp
from jax import lax
from jax.experimental import pallas as pl
from jax.experimental.pallas import tpu as pltpu
from jax.sharding import PartitionSpec as P

MESH = pl.DeviceIdType.MESH
SINE = (4.4415356787207045, -7.2646801556685014, 3.252047353220934)
COSINE = (1.414204078817102, -6.977641981219209, 5.715237646584958, -1.728346667500456)


def node_points(node_index, node_count):
    angles = 2.0 * math.pi / node_count * (node_index.astype(jnp.float32) + 0.5)
    radius = 1.0 + 0.25 * jnp.cos(3.0 * angles)
    return (radius * jnp.cos(angles), radius * jnp.sin(angles))


def kernel_block(rows, wide, step, row_x, row_y, col_x, col_y, weights, scale, out, parts):
    @pl.loop(0, rows // step)
    def _(index):
        here = pl.ds(pl.multiple_of(index * step, step), step)
        below = pl.ds(pl.multiple_of(rows + index * step, step), step)
        x, y = row_x[here, :], row_y[here, :]
        for first in range(0, wide, 128):
            lanes = slice(first, first + 128)
            dx = x - col_x[0:1, lanes]
            dy = y - col_y[0:1, lanes]
            square = jnp.maximum(dx * dx + dy * dy, 1e-30)
            turns = square * lax.rsqrt(square)
            part = turns - jnp.round(turns)
            amplitude = lax.rsqrt(turns + 0.5 / math.pi)
            z = part * part
            sine = part * (SINE[0] + z * (SINE[1] + z * SINE[2]))
            cosine = COSINE[0] + z * (COSINE[1] + z * (COSINE[2] + z * COSINE[3]))
            scaled = amplitude * sine
            parts[here, lanes] = (amplitude - scaled * sine).astype(jnp.bfloat16)
            parts[below, lanes] = (scaled * cosine).astype(jnp.bfloat16)

    both = jnp.dot(parts[...], weights[...], preferred_element_type=jnp.float32)
    half = both.shape[1] // 2
    crossed = both[rows:]
    product = both[:rows] + jnp.concatenate([-crossed[:, half:], crossed[:, :half]], axis=1)
    product = product * scale[...]

    @pl.when(pl.program_id(1) == 0)
    def _():
        out[...] = product

    @pl.when(pl.program_id(1) > 0)
    def _():
        out[...] += product


def sketch_rows(row_first, impedance_rows, column_ids, omega_rows, node_count):
    rows, columns = impedance_rows.shape[0], column_ids.shape[0]
    row_block, wide, step = 512, 1024, 32
    width = omega_rows.shape[1]
    turn = node_count / 16.0 / (2.0 * math.pi)
    col_x, col_y = node_points(column_ids, node_count)
    row_x, row_y = node_points(row_first + jnp.arange(rows, dtype=jnp.int32), node_count)
    spread = lambda v: jnp.broadcast_to(v[:, None], (rows, 128))
    row_spec = pl.BlockSpec((row_block, 128), lambda i, j: (i, 0))
    col_spec = pl.BlockSpec((1, wide), lambda i, j: (0, j))
    return pl.pallas_call(
        functools.partial(kernel_block, row_block, wide, step),
        grid=(rows // row_block, columns // wide),
        in_specs=[
            row_spec,
            row_spec,
            col_spec,
            col_spec,
            pl.BlockSpec((wide, width), lambda i, j: (j, 0)),
            row_spec,
        ],
        out_specs=pl.BlockSpec((row_block, width), lambda i, j: (i, 0)),
        out_shape=jax.ShapeDtypeStruct((rows, width), jnp.float32),
        scratch_shapes=[pltpu.VMEM((2 * row_block, wide), jnp.bfloat16)],
        compiler_params=pltpu.CompilerParams(vmem_limit_bytes=40 << 20),
    )(
        spread(row_x * turn),
        spread(row_y * turn),
        (col_x * turn)[None],
        (col_y * turn)[None],
        omega_rows,
        spread(impedance_rows / math.sqrt(2.0 * math.pi)),
    )


def split(values, axis, order):
    high = values.astype(jnp.bfloat16)
    rest = values - high.astype(jnp.float32)
    middle = rest.astype(jnp.bfloat16)
    low = (rest - middle.astype(jnp.float32)).astype(jnp.bfloat16)
    pieces = (high, middle, low)
    return jnp.concatenate([pieces[i] for i in order], axis=axis)


LEFT, RIGHT = (0, 0, 1, 0, 1, 2), (0, 1, 0, 2, 1, 0)


def product(first, second, first_axis=1, second_axis=0):
    return lax.dot_general(
        split(first, first_axis, LEFT),
        split(second, second_axis, RIGHT),
        (((first_axis,), (second_axis,)), ((), ())),
        preferred_element_type=jnp.float32,
    )


def spread_rows(row, count):
    return jnp.broadcast_to(row, (count, row.shape[1]))


def eliminate_panel(panel, first, lanes):
    pieces = panel.shape[0] // 8
    rows = [panel[8 * i : 8 * i + 8] for i in range(pieces)]
    sublane = lax.broadcasted_iota(jnp.int32, (8, lanes), 0)
    twice = lambda v: jnp.concatenate([v, v], axis=1)
    done = []
    for top in range(pieces):
        columns = [
            [
                jnp.take_along_axis(
                    rows[i][:, :lanes],
                    jnp.full((8, lanes), first + 8 * top + t, jnp.int32),
                    axis=1,
                )
                for i in range(top, pieces)
            ]
            for t in range(8)
        ]
        for t in range(8):
            pivot = spread_rows(columns[t][0][t : t + 1], 8)
            inverse = 1.0 / pivot
            row = rows[top][t : t + 1]
            done.append(row * twice(lax.rsqrt(pivot[0:1])))
            factors = [c * inverse for c in columns[t]]
            factors[0] = jnp.where(sublane > t, factors[0], 0.0)
            for u in range(t + 1, 8):
                entry = spread_rows(columns[u][0][t : t + 1], 8)
                columns[u] = [c - f * entry for c, f in zip(columns[u], factors)]
            full_row = spread_rows(row, 8)
            for i, f in enumerate(factors):
                rows[top + i] = rows[top + i] - twice(f) * full_row
    return jnp.concatenate(done, axis=0)


def factor_solve(gram_matrix, right):
    size, block = gram_matrix.shape[0], 32
    diagonal = lax.broadcasted_iota(jnp.int32, (size, size), 0) == lax.broadcasted_iota(
        jnp.int32, (size, size), 1
    )
    trace = jnp.sum(jnp.where(diagonal, gram_matrix, 0.0), axis=(0, 1), keepdims=True)
    shifted = gram_matrix + jnp.where(diagonal, 0.25 * trace / size + 1e-06, 0.0)
    rest = jnp.concatenate([shifted, right], axis=1)
    solved = []
    for first in range(0, size, block):
        panel = eliminate_panel(rest[:block], first, size)
        solved.append(panel[:, size:])
        if first + block < size:
            rest = rest[block:] - product(panel[:, :size], panel, 0, 0)[first + block :]
    return jnp.concatenate(solved, axis=0)


def merge_kernel(rows, sketch, maps, out, sends, gots, send_sems, got_sems):
    src, tgt = lax.axis_index("src"), lax.axis_index("tgt")
    mates = (
        tgt + 1 - 2 * (tgt % 2),
        tgt + 2 - 4 * ((tgt // 2) % 2),
        tgt + 3 - 2 * (tgt % 4),
        tgt + 4 - 8 * ((tgt // 4) % 2),
    )
    barrier = pltpu.get_barrier_semaphore()
    for mate in mates:
        pl.semaphore_signal(barrier, inc=1, device_id=(src, mate), device_id_type=MESH)
    pl.semaphore_wait(barrier, len(mates))

    copies = []

    def post(values, targets):
        source = sends.at[sum(len(c) > 0 for c in copies)]
        source[...] = values
        base = sum(len(c) for c in copies)
        batch = []
        for i, target in enumerate(targets):
            copy = pltpu.make_async_remote_copy(
                src_ref=source,
                dst_ref=gots.at[base + i],
                send_sem=send_sems.at[base + i],
                recv_sem=got_sems.at[base + i],
                device_id=(src, mates[target]),
                device_id_type=MESH,
            )
            copy.start()
            batch.append((copy, base + i))
        copies.append(batch)
        return batch

    def take(batch):
        values = []
        for copy, slot in batch:
            copy.wait_recv()
            values.append(gots[slot])
        return values

    cross = lax.dot_general(
        sketch[...], sketch[...], (((0,), (0,)), ((), ())), preferred_element_type=jnp.float32
    )
    wide_maps = [maps[k].astype(jnp.float32) for k in range(4)]
    images = [product(cross, m) for m in wide_maps]
    gram_matrix = product(wide_maps[0], images[0], 0, 0) / rows
    turned = factor_solve(gram_matrix, wide_maps[0].T)
    for level in range(3):
        part = product(turned, images[level + 1]) / (rows * 2**level)
        if level == 0:
            batch = post(part, (0,))
            own = part
        else:
            batch = post(part, (0, 1, 2))
            near, far, beyond = take(batch)
            own = part + near
            if level == 1:
                other = far + beyond
            else:
                own = own + (far + beyond)
                batch = post(own, (3,))
        mine = product(own, own, 0, 0)
        right = product(own, turned, 0, 0)
        if level != 1:
            (other,) = take(batch)
        gram_matrix = (mine + product(other, other, 0, 0)) / 2.0
        turned = factor_solve(gram_matrix, right)
    for batch in copies:
        for copy, _ in batch:
            copy.wait_send()
    turned = split(turned, 1, (0, 1, 2))
    sketch_here = sketch[...]
    out[...] = lax.dot_general(
        jnp.concatenate([sketch_here] * 3, axis=1),
        turned,
        (((1,), (1,)), ((), ())),
        preferred_element_type=jnp.float32,
    )


def merged_bases(sketch, maps_here):
    rows, width = sketch.shape
    tile = (width, width)
    return pl.pallas_call(
        functools.partial(merge_kernel, rows),
        out_shape=jax.ShapeDtypeStruct((rows, width), jnp.float32),
        in_specs=[pl.BlockSpec(memory_space=pltpu.VMEM)] * 2,
        out_specs=pl.BlockSpec(memory_space=pltpu.VMEM),
        scratch_shapes=[
            pltpu.VMEM((4, *tile), jnp.float32),
            pltpu.VMEM((8, *tile), jnp.float32),
            pltpu.SemaphoreType.DMA((8,)),
            pltpu.SemaphoreType.DMA((8,)),
        ],
        compiler_params=pltpu.CompilerParams(
            collective_id=0, has_side_effects=True, vmem_limit_bytes=40 << 20
        ),
    )(sketch, maps_here)


def per_device(omega, owners, columns, impedance, level_maps):
    sample_count = omega.shape[0]
    device_count = lax.axis_size(("src", "tgt"))
    tgt_count = lax.axis_size("tgt")
    capacity = 2 * sample_count // device_count
    owner_list = owners[:, 0]
    onehot = (owner_list[:, None] == jnp.arange(device_count, dtype=jnp.int32)[None, :]).astype(
        jnp.int32
    )
    earlier = jnp.cumsum(onehot, axis=0) - onehot
    slot_rank = jnp.sum(earlier * onehot, axis=1)
    position = owner_list * capacity + slot_rank
    send_rows = (
        jnp.zeros((device_count * capacity, omega.shape[1]), omega.dtype).at[position].set(omega)
    )
    send_ids = jnp.zeros((device_count * capacity,), jnp.int32).at[position].set(columns)
    got_rows, got_ids = (
        lax.all_to_all(
            send_rows.reshape(device_count, capacity, omega.shape[1]),
            ("src", "tgt"),
            split_axis=0,
            concat_axis=0,
            tiled=True,
        ),
        lax.all_to_all(
            send_ids.reshape(device_count, capacity),
            ("src", "tgt"),
            split_axis=0,
            concat_axis=0,
            tiled=True,
        ),
    )
    slot_rows = got_rows.reshape(device_count * capacity, omega.shape[1])
    slot_ids = got_ids.reshape(device_count * capacity)
    row_count = impedance.shape[0]
    node_count = tgt_count * row_count
    tgt_place = lax.axis_index("tgt")
    sketch = sketch_rows(tgt_place * row_count, impedance, slot_ids, slot_rows, node_count).astype(
        jnp.bfloat16
    )
    maps_here = level_maps[0]
    return merged_bases(sketch, maps_here)[None]


def solution(mesh):
    in_specs = (
        P(("src", "tgt"), None),
        P(("src", "tgt"), None),
        P(("src", "tgt")),
        P("tgt"),
        P("src", None, None, None),
    )
    out_specs = P("src", "tgt", None)
    return jax.shard_map(
        per_device, mesh=mesh, in_specs=in_specs, out_specs=out_specs, check_vma=False
    )
```

profile of v0, /device:TPU:10, one launch (start us, length us, event | category | flops | bytes accessed | tf_op | source)
XLA Modules:
  0.0 193.5 jit_solution(16434348227818546399)
XLA Ops:
  0.0 0.8 copy.12
  0.8 0.6 fusion.2
  1.4 0.1 reduce-window.9
  1.5 0.2 broadcast_add_fusion
  1.7 0.0 copy-start.1
  1.7 1.2 copy.13
  3.0 0.0 copy-done.1
  3.0 1.4 fusion.1
  4.5 15.7 %scatter_custom_fusion = s32[8192]{0:T(1024)S(1)} fusion(s32[4096]{0:T(1024)S(1)} %bitcast.30, s32[4096]{0:T(1024)} %param.7, s32[]{:T(128)} %constant.21.clone.1), kind=kCustom, calls=%fused_computation.20 | custom fusion | bytes 33280 | tf_op jit(solution)/shard_map/scatter | solution.py:285
  20.2 0.7 all_to_all.9
  20.9 10.4 %all-to-all-start = ((s32[128,1,64]{2,1,0:T(1,128)}), s32[128,1,64]{2,1,0:T(1,128)S(1)}, u32[]{:S(2)}, u32[]{:S(2)}) async-start(s32[128,1,64]{2,1,0:T(1,128)} %bitcast.7), calls=%async_computation | async-start | bytes 131072 | tf_op jit(solution)/shard_map/all_to_all | solution.py:294
  31.3 12.8 %scatter_custom_fusion.1 = bf16[8192,128]{1,0:T(8,128)(2,1)} fusion(s32[4096]{0:T(1024)S(1)} %bitcast.31, bf16[4096,128]{1,0:T(8,128)(2,1)} %param.5, bf16[]{:T(256)} %constant.8.clone.1), kind=kCustom, calls=%fused_computation.9 | custom fusion | bytes 2097664 | tf_op jit(solution)/shard_map/scatter | solution.py:283
  44.1 0.0 all-to-all-done
  44.1 0.0 copy-start.2
  44.1 9.8 %all-to-all-start.1 = ((bf16[128,64,128]{2,1,0:T(8,128)(2,1)}), bf16[128,64,128]{2,1,0:T(8,128)(2,1)S(1)}, u32[]{:S(2)}, u32[]{:S(2)}) async-start(bf16[128,64,128]{2,1,0:T(8,128)(2,1)} %bitcast.26), calls=%async_computation.1 | async-start | bytes 4194304 | tf_op jit(solution)/shard_map/all_to_all | solution.py:287
  53.9 0.1 multiply_multiply_fusion.2
  54.0 0.0 copy-done.2
  54.0 0.1 copy.15
  54.1 0.3 multiply_multiply_fusion
  54.3 0.1 copy.16
  54.4 0.1 reshape.120.col_x
  54.5 0.1 copy.17
  54.6 0.1 reshape.122.col_y
  54.7 28.0 %all-to-all-done.1 = bf16[128,64,128]{2,1,0:T(8,128)(2,1)S(1)} async-done(((bf16[128,64,128]{2,1,0:T(8,128)(2,1)}), bf16[128,64,128]{2,1,0:T(8,128)(2,1)S(1)}, u32[]{:S(2)}, u32[]{:S(2)}) %all-to-all-start.1) | async-done | bytes 2097184 | tf_op jit(solution)/shard_map/all_to_all | solution.py:287
  82.7 0.3 broadcast_in_dim.12.row_x
  83.0 0.3 broadcast_in_dim.13.row_y
  83.3 0.3 broadcast_in_dim.16.scale
  83.5 0.0 copy-start
  83.5 74.4 %shard_map.55 = f32[1536,128]{1,0:T(8,128)S(1)} custom-call(f32[1536,128]{1,0:T(8,128)S(1)} %broadcast_in_dim.12.row_x, f32[1536,128]{1,0:T(8,128)S(1)} %broadcast_in_dim.13.row_y, f32[1,8192]{1,0:T(1,128)S(1)} %reshape.120.col_x, f32[1,8192]{1,0:T(1,128)S(1)} %reshape.122.col_y, bf16[8192,128]{1,0:T(8,128)(2,1)S(1)} %bitcast.23, ...), custom_call_target="tpu_custom_call" | custom-call | tf_op jit(solution)/shard_map/pallas_call | solution.py:68
  158.0 0.0 copy-done
  158.0 34.7 %shard_map.56 = f32[1536,128]{1,0:T(8,128)S(1)} custom-call(bf16[1536,128]{1,0:T(8,128)(2,1)S(1)} %convert_element_type.39.sketch, bf16[4,128,128]{2,1,0:T(8,128)(2,1)S(1)} %bitcast.25), custom_call_target="tpu_custom_call" | custom-call | tf_op jit(solution)/shard_map/pallas_call | solution.py:253
  192.6 0.9 copy.19
  (5 shorter events, 0.1 us)
Async XLA Ops:
  1.7 1.2 copy-start.1
  20.9 23.2 %all-to-all-start = ((s32[128,1,64]{2,1,0:T(1,128)}), s32[128,1,64]{2,1,0:T(1,128)S(1)}, u32[]{:S(2)}, u32[]{:S(2)}) async-start(s32[128,1,64]{2,1,0:T(1,128)} %bitcast.7), calls=%async_computation | async-start | bytes 131072 | tf_op jit(solution)/shard_map/all_to_all | solution.py:294
  44.1 9.9 %copy-start.2 = (f32[1536]{0:T(1024)S(1)}, f32[1536]{0:T(1024)}, u32[]{:S(2)}) copy-start(f32[1536]{0:T(1024)} %param.8) | copy-start | bytes 18436
  44.1 38.6 %all-to-all-start.1 = ((bf16[128,64,128]{2,1,0:T(8,128)(2,1)}), bf16[128,64,128]{2,1,0:T(8,128)(2,1)S(1)}, u32[]{:S(2)}, u32[]{:S(2)}) async-start(bf16[128,64,128]{2,1,0:T(8,128)(2,1)} %bitcast.26), calls=%async_computation.1 | async-start | bytes 4194304 | tf_op jit(solution)/shard_map/all_to_all | solution.py:287
  83.5 74.5 %copy-start = (bf16[1,4,128,128]{3,2,1,0:T(8,128)(2,1)S(1)}, bf16[1,4,128,128]{3,2,1,0:T(8,128)(2,1)}, u32[]{:S(2)}) copy-start(bf16[1,4,128,128]{3,2,1,0:T(8,128)(2,1)} %param.9) | copy-start | bytes 393220
where the time goes:
time: 195 us; the launch traced here: 194 us
  Pallas kernels  109 us (56%)
  local copies, waits for them, and re-layouts  33.4 us (17%)
  waiting for transfers between devices  28 us (14%)
  starting transfers between devices  20.2 us (10%)
  other arithmetic  2.74 us (1%)
    pallas_call x1, Pallas kernels, sketch_rows(): pl.pallas_call(functools.partial(kernel_block, row_block, wide, step), gr...  74.4 us
    pallas_call x1, Pallas kernels, merged_bases(): pl.pallas_call(functools.partial(merge_kernel, rows), out_shape=jax.Shape...  34.7 us
    all_to_all x1, waiting for transfers between devices, per_device(): lax.all_to_all(send_rows.reshape(device_count, capacity, omega.shape[1]),...  28 us
    scatter x1, local copies, waits for them, and re-layouts, per_device(): jnp.zeros((device_count * capacity,), jnp.int32).at[position].set(columns)  15.7 us
    scatter x1, local copies, waits for them, and re-layouts, per_device(): jnp.zeros((device_count * capacity, omega.shape[1]), omega.dtype)  12.8 us
    all_to_all x1, starting transfers between devices, per_device(): lax.all_to_all(send_ids.reshape(device_count, capacity), ('src', 'tgt'),...  10.4 us
    all_to_all x1, starting transfers between devices, per_device(): lax.all_to_all(send_rows.reshape(device_count, capacity, omega.shape[1]),...  9.77 us
  transfers between devices with their start and end apart: 2, of which 1 were waited for; matrix products, arithmetic and copies ran while one was open for 7% of the time, Pallas kernels for 0%

commit v1 on v0

--- a/solution.py
+++ b/solution.py
@@ -19,73 +19,235 @@
     return (radius * jnp.cos(angles), radius * jnp.sin(angles))
 
 
-def kernel_block(rows, wide, step, row_x, row_y, col_x, col_y, weights, scale, out, parts):
-    @pl.loop(0, rows // step)
-    def _(index):
-        here = pl.ds(pl.multiple_of(index * step, step), step)
-        below = pl.ds(pl.multiple_of(rows + index * step, step), step)
-        x, y = row_x[here, :], row_y[here, :]
-        for first in range(0, wide, 128):
-            lanes = slice(first, first + 128)
-            dx = x - col_x[0:1, lanes]
-            dy = y - col_y[0:1, lanes]
-            square = jnp.maximum(dx * dx + dy * dy, 1e-30)
-            turns = square * lax.rsqrt(square)
-            part = turns - jnp.round(turns)
-            amplitude = lax.rsqrt(turns + 0.5 / math.pi)
-            z = part * part
-            sine = part * (SINE[0] + z * (SINE[1] + z * SINE[2]))
-            cosine = COSINE[0] + z * (COSINE[1] + z * (COSINE[2] + z * COSINE[3]))
-            scaled = amplitude * sine
-            parts[here, lanes] = (amplitude - scaled * sine).astype(jnp.bfloat16)
-            parts[below, lanes] = (scaled * cosine).astype(jnp.bfloat16)
-
-    both = jnp.dot(parts[...], weights[...], preferred_element_type=jnp.float32)
-    half = both.shape[1] // 2
-    crossed = both[rows:]
-    product = both[:rows] + jnp.concatenate([-crossed[:, half:], crossed[:, :half]], axis=1)
-    product = product * scale[...]
-
-    @pl.when(pl.program_id(1) == 0)
-    def _():
-        out[...] = product
-
-    @pl.when(pl.program_id(1) > 0)
-    def _():
-        out[...] += product
-
-
-def sketch_rows(row_first, impedance_rows, column_ids, omega_rows, node_count):
-    rows, columns = impedance_rows.shape[0], column_ids.shape[0]
-    row_block, wide, step = 512, 1024, 32
-    width = omega_rows.shape[1]
+def thirds(values):
+    high = values.astype(jnp.bfloat16)
+    rest = values - high.astype(jnp.float32)
+    middle = rest.astype(jnp.bfloat16)
+    low = (rest - middle.astype(jnp.float32)).astype(jnp.bfloat16)
+    return high, middle, low
+
+
+def pack_kernel(
+    capacity, owners, col_x, col_y, omega, rows_out, points_out, places, placed, table, wide, plain, sem
+):
+    blocks, lanes = owners.shape
+    count = points_out.shape[0]
+    owner_at = lax.broadcasted_iota(jnp.int32, (count, lanes), 0)
+    before = (
+        lax.broadcasted_iota(jnp.int32, (lanes, lanes), 0)
+        < lax.broadcasted_iota(jnp.int32, (lanes, lanes), 1)
+    ).astype(jnp.float32).astype(jnp.bfloat16)
+    ones = jnp.ones((lanes, lanes), jnp.bfloat16)
+    rank_at = lax.broadcasted_iota(jnp.int32, (capacity, lanes), 0)
+    wide[...] = jnp.zeros_like(wide)
+    table[...] = jnp.zeros_like(table)
+    plain[...] = omega[...].astype(jnp.float32)
+
+    def one_block(index, running):
+        here = pl.ds(index, 1)
+        owner = owners[here, :]
+        named = owner_at == owner
+        onehot = named.astype(jnp.float32).astype(jnp.bfloat16)
+        earlier = jnp.dot(onehot, before, preferred_element_type=jnp.float32) + running
+        rank = jnp.sum(jnp.where(named, earlier, 0.0), axis=0, keepdims=True).astype(jnp.int32)
+        places[here, :] = owner * capacity + rank
+        ranked = rank_at == rank
+        pieces = [
+            jnp.where(ranked, piece.astype(jnp.float32), 0.0).astype(jnp.bfloat16)
+            for values in (col_x[here, :], col_y[here, :])
+            for piece in thirds(values)
+        ]
+        table[...] += lax.dot_general(
+            onehot,
+            jnp.concatenate(pieces, axis=0),
+            (((1,), (1,)), ((), ())),
+            preferred_element_type=jnp.float32,
+        )
+        return running + jnp.dot(onehot, ones, preferred_element_type=jnp.float32)
+
+    lax.fori_loop(0, blocks, one_block, jnp.zeros((count, lanes), jnp.float32), unroll=4)
+    copy = pltpu.make_async_copy(places, placed, sem)
+    copy.start()
+    sums = table[...]
+    piece = [sums[:, i * capacity : (i + 1) * capacity] for i in range(6)]
+    points_out[...] = jnp.concatenate(
+        [(piece[2] + piece[1]) + piece[0], (piece[5] + piece[4]) + piece[3]], axis=1
+    )
+    copy.wait()
+
+    @pl.loop(0, blocks)
+    def _(block):
+        @pl.loop(0, lanes // 32)
+        def _(part):
+            for lane in range(32):
+                at = part * 32 + lane
+                wide[pl.ds(placed[block, at], 1), :] = plain[pl.ds(block * lanes + at, 1), :]
+
+    rows_out[...] = wide[...].astype(jnp.bfloat16)
+
+
+def packed_slots(omega, owners, columns, count, node_count):
+    samples, width = omega.shape
+    lanes = 128
+    blocks = samples // lanes
+    capacity = 2 * samples // count
     turn = node_count / 16.0 / (2.0 * math.pi)
-    col_x, col_y = node_points(column_ids, node_count)
+    col_x, col_y = node_points(columns.reshape(blocks, lanes), node_count)
+    vmem = pl.BlockSpec(memory_space=pltpu.VMEM)
+    return pl.pallas_call(
+        functools.partial(pack_kernel, capacity),
+        out_shape=(
+            jax.ShapeDtypeStruct((count * capacity, width), jnp.bfloat16),
+            jax.ShapeDtypeStruct((count, 2 * capacity), jnp.float32),
+        ),
+        in_specs=[vmem] * 4,
+        out_specs=(vmem, vmem),
+        scratch_shapes=[
+            pltpu.VMEM((blocks, lanes), jnp.int32),
+            pltpu.SMEM((blocks, lanes), jnp.int32),
+            pltpu.VMEM((count, 6 * capacity), jnp.float32),
+            pltpu.VMEM((count * capacity, width), jnp.float32),
+            pltpu.VMEM((samples, width), jnp.float32),
+            pltpu.SemaphoreType.DMA,
+        ],
+        compiler_params=pltpu.CompilerParams(vmem_limit_bytes=40 << 20),
+    )(owners.reshape(blocks, lanes), col_x * turn, col_y * turn, omega)
+
+
+def kernel_values(x, y, col_x, col_y):
+    dx = x - col_x
+    dy = y - col_y
+    square = jnp.maximum(dx * dx + dy * dy, 1e-30)
+    turns = square * lax.rsqrt(square)
+    part = turns - jnp.round(turns)
+    amplitude = lax.rsqrt(turns + 0.5 / math.pi)
+    z = part * part
+    sine = part * (SINE[0] + z * (SINE[1] + z * SINE[2]))
+    cosine = COSINE[0] + z * (COSINE[1] + z * (COSINE[2] + z * COSINE[3]))
+    scaled = amplitude * sine
+    return (amplitude - scaled * sine).astype(jnp.bfloat16), (scaled * cosine).astype(jnp.bfloat16)
+
+
+def sketch_kernel(
+    shape, slots, points, row_x, row_y, scale, out, got, got_points, cols, parts, total, sent, got_sems
+):
+    src_count, tgt_count = shape
+    src, tgt = lax.axis_index("src"), lax.axis_index("tgt")
+    rows, lanes = row_x.shape
+    capacity, width = slots.shape[1:]
+    chunk, step = 512, 32
+    columns = tgt_count * capacity
+
+    def device(offset):
+        return (
+            (src + offset // tgt_count) % src_count,
+            (tgt + offset % tgt_count) % tgt_count,
+        )
+
+    barrier = pltpu.get_barrier_semaphore()
+
+    @pl.loop(1, src_count * tgt_count)
+    def _(offset):
+        pl.semaphore_signal(barrier, inc=1, device_id=device(offset), device_id_type=MESH)
+
+    me = src * tgt_count + tgt
+    pltpu.make_async_copy(points.at[me], got_points.at[0, 0], got_sems.at[0, 0]).start()
+    pltpu.make_async_copy(slots.at[me], got.at[0, 0], got_sems.at[1, 0]).start()
+    pl.semaphore_wait(barrier, src_count * tgt_count - 1)
+
+    @pl.loop(1, src_count * tgt_count)
+    def _(offset):
+        there = device(offset)
+        owner = there[0] * tgt_count + there[1]
+        group, place = offset // tgt_count, offset % tgt_count
+        for kind, (source, target) in enumerate(((points, got_points), (slots, got))):
+            pltpu.make_async_remote_copy(
+                src_ref=source.at[owner],
+                dst_ref=target.at[group, place],
+                send_sem=sent.at[kind],
+                recv_sem=got_sems.at[kind, group],
+                device_id=there,
+                device_id_type=MESH,
+            ).start()
+
+    total[...] = jnp.zeros_like(total)
+
+    @pl.loop(0, src_count)
+    def _(group):
+        pltpu.make_async_copy(got_points.at[group], got_points.at[group], got_sems.at[0, group]).wait()
+        pairs = got_points[group].reshape(tgt_count, lanes)
+        col_x = [
+            jnp.concatenate([pairs[i : i + 1, :capacity], pairs[i + 1 : i + 2, :capacity]], axis=1)
+            for i in range(0, tgt_count, 2)
+        ]
+        col_y = [
+            jnp.concatenate([pairs[i : i + 1, capacity:], pairs[i + 1 : i + 2, capacity:]], axis=1)
+            for i in range(0, tgt_count, 2)
+        ]
+        for i in range(tgt_count // 2):
+            cols[0:1, i * lanes : (i + 1) * lanes] = col_x[i]
+            cols[1:2, i * lanes : (i + 1) * lanes] = col_y[i]
+        pltpu.make_async_copy(got.at[group], got.at[group], got_sems.at[1, group]).wait()
+
+        @pl.loop(0, rows // chunk)
+        def _(part):
+            @pl.loop(0, chunk // step)
+            def _(index):
+                here = pl.ds(pl.multiple_of(part * chunk + index * step, step), step)
+                x, y = row_x[here, :], row_y[here, :]
+                real_at = pl.ds(pl.multiple_of(index * step, step), step)
+                imag_at = pl.ds(pl.multiple_of(chunk + index * step, step), step)
+                for first in range(0, columns, lanes):
+                    at = slice(first, first + lanes)
+                    real, imag = kernel_values(x, y, cols[0:1, at], cols[1:2, at])
+                    parts[real_at, at] = real
+                    parts[imag_at, at] = imag
+
+            weights = got[group].reshape(columns, width)
+            both = jnp.dot(parts[...], weights, preferred_element_type=jnp.float32)
+            crossed = both[chunk:]
+            half = width // 2
+            here = pl.ds(pl.multiple_of(part * chunk, chunk), chunk)
+            total[here, :] += both[:chunk] + jnp.concatenate(
+                [-crossed[:, half:], crossed[:, :half]], axis=1
+            )
+
+    out[...] = (total[...] * scale[...]).astype(jnp.bfloat16)
+    rest = pl.ds(0, src_count * tgt_count - 1)
+    for kind, source in enumerate((points, slots)):
+        pltpu.make_async_copy(source.at[rest], source.at[rest], sent.at[kind]).wait()
+
+
+def sketch_rows(row_first, impedance_rows, slots, points, mesh_shape, node_count):
+    rows = impedance_rows.shape[0]
+    count, capacity, width = slots.shape
+    turn = node_count / 16.0 / (2.0 * math.pi)
     row_x, row_y = node_points(row_first + jnp.arange(rows, dtype=jnp.int32), node_count)
     spread = lambda v: jnp.broadcast_to(v[:, None], (rows, 128))
-    row_spec = pl.BlockSpec((row_block, 128), lambda i, j: (i, 0))
-    col_spec = pl.BlockSpec((1, wide), lambda i, j: (0, j))
+    columns = mesh_shape[1] * capacity
+    vmem = pl.BlockSpec(memory_space=pltpu.VMEM)
     return pl.pallas_call(
-        functools.partial(kernel_block, row_block, wide, step),
-        grid=(rows // row_block, columns // wide),
-        in_specs=[
-            row_spec,
-            row_spec,
-            col_spec,
-            col_spec,
-            pl.BlockSpec((wide, width), lambda i, j: (j, 0)),
-            row_spec,
+        functools.partial(sketch_kernel, mesh_shape),
+        out_shape=jax.ShapeDtypeStruct((rows, width), jnp.bfloat16),
+        in_specs=[vmem] * 5,
+        out_specs=vmem,
+        scratch_shapes=[
+            pltpu.VMEM((*mesh_shape, capacity, width), jnp.bfloat16),
+            pltpu.VMEM((*mesh_shape, 1, 2 * capacity), jnp.float32),
+            pltpu.VMEM((8, columns), jnp.float32),
+            pltpu.VMEM((1024, columns), jnp.bfloat16),
+            pltpu.VMEM((rows, width), jnp.float32),
+            pltpu.SemaphoreType.DMA((2,)),
+            pltpu.SemaphoreType.DMA((2, mesh_shape[0])),
         ],
-        out_specs=pl.BlockSpec((row_block, width), lambda i, j: (i, 0)),
-        out_shape=jax.ShapeDtypeStruct((rows, width), jnp.float32),
-        scratch_shapes=[pltpu.VMEM((2 * row_block, wide), jnp.bfloat16)],
-        compiler_params=pltpu.CompilerParams(vmem_limit_bytes=40 << 20),
+        compiler_params=pltpu.CompilerParams(
+            collective_id=1, has_side_effects=True, vmem_limit_bytes=48 << 20
+        ),
     )(
+        slots,
+        points,
         spread(row_x * turn),
         spread(row_y * turn),
-        (col_x * turn)[None],
-        (col_y * turn)[None],
-        omega_rows,
         spread(impedance_rows / math.sqrt(2.0 * math.pi)),
     )
 
@@ -268,47 +430,20 @@
 
 
 def per_device(omega, owners, columns, impedance, level_maps):
-    sample_count = omega.shape[0]
-    device_count = lax.axis_size(("src", "tgt"))
-    tgt_count = lax.axis_size("tgt")
-    capacity = 2 * sample_count // device_count
-    owner_list = owners[:, 0]
-    onehot = (owner_list[:, None] == jnp.arange(device_count, dtype=jnp.int32)[None, :]).astype(
-        jnp.int32
-    )
-    earlier = jnp.cumsum(onehot, axis=0) - onehot
-    slot_rank = jnp.sum(earlier * onehot, axis=1)
-    position = owner_list * capacity + slot_rank
-    send_rows = (
-        jnp.zeros((device_count * capacity, omega.shape[1]), omega.dtype).at[position].set(omega)
-    )
-    send_ids = jnp.zeros((device_count * capacity,), jnp.int32).at[position].set(columns)
-    got_rows, got_ids = (
-        lax.all_to_all(
-            send_rows.reshape(device_count, capacity, omega.shape[1]),
-            ("src", "tgt"),
-            split_axis=0,
-            concat_axis=0,
-            tiled=True,
-        ),
-        lax.all_to_all(
-            send_ids.reshape(device_count, capacity),
-            ("src", "tgt"),
-            split_axis=0,
-            concat_axis=0,
-            tiled=True,
-        ),
-    )
-    slot_rows = got_rows.reshape(device_count * capacity, omega.shape[1])
-    slot_ids = got_ids.reshape(device_count * capacity)
-    row_count = impedance.shape[0]
-    node_count = tgt_count * row_count
-    tgt_place = lax.axis_index("tgt")
-    sketch = sketch_rows(tgt_place * row_count, impedance, slot_ids, slot_rows, node_count).astype(
-        jnp.bfloat16
-    )
-    maps_here = level_maps[0]
-    return merged_bases(sketch, maps_here)[None]
+    mesh_shape = (lax.axis_size("src"), lax.axis_size("tgt"))
+    count = mesh_shape[0] * mesh_shape[1]
+    rows = impedance.shape[0]
+    node_count = mesh_shape[1] * rows
+    slots, points = packed_slots(omega, owners, columns, count, node_count)
+    sketch = sketch_rows(
+        lax.axis_index("tgt") * rows,
+        impedance,
+        slots.reshape(count, -1, slots.shape[1]),
+        points.reshape(count, 1, -1),
+        mesh_shape,
+        node_count,
+    )
+    return merged_bases(sketch, level_maps[0])[None]
 
 
 def solution(mesh):

time: 195 us -> 163 us (0.84)
  Pallas kernels: 109 us -> 160 us
  local copies, waits for them, and re-layouts: 33.4 us -> 1.68 us
  waiting for transfers between devices: 28 us -> 0 us
  starting transfers between devices: 20.2 us -> 0 us
    pallas_call x1 -> x2, Pallas kernels: 74.4 us -> 123 us  [the longest x1 104 us: sketch_rows(): pl.pallas_call(functools.partial(sketch_kernel, mesh_shape), out_shape=ja...]
    scatter x2 -> x0, local copies, waits for them, and re-layouts: 28.5 us -> none  [the longest x1 15.7 us: per_device(): jnp.zeros((device_count * capacity,), jnp.int32).at[position].set(columns)]
    all_to_all x2 -> x0, waiting for transfers between devices: 28 us -> none  [the longest x1 28 us: per_device(): lax.all_to_all(send_rows.reshape(device_count, capacity, omega.shape[1]),...]
    all_to_all x2 -> x0, starting transfers between devices: 20.2 us -> none  [the longest x1 10.4 us: per_device(): lax.all_to_all(send_ids.reshape(device_count, capacity), ('src', 'tgt'),...]
    pallas_call x1, Pallas kernels: 34.7 us -> 37.1 us  [merged_bases(): pl.pallas_call(functools.partial(merge_kernel, rows), out_shape=jax.Shape...]
  transfers between devices with their start and end apart: 2 -> 0, of which waited for: 1 -> 0; matrix products, arithmetic and copies ran while one was open for 7% -> 0% of each run, Pallas kernels for 0% -> 0%
where the time goes in v1:
time: 163 us
  Pallas kernels  160 us (98%)
  other arithmetic  1.72 us (1%)
  local copies, waits for them, and re-layouts  1.68 us (1%)
    pallas_call x1, Pallas kernels, sketch_rows(): pl.pallas_call(functools.partial(sketch_kernel, mesh_shape), out_shape=ja...  104 us
    pallas_call x1, Pallas kernels, merged_bases(): pl.pallas_call(functools.partial(merge_kernel, rows), out_shape=jax.Shape...  37.1 us
    pallas_call x1, Pallas kernels, packed_slots(): pl.pallas_call(functools.partial(pack_kernel, capacity), out_shape=(jax.S...  19 us

profile of v1, /device:TPU:10, one launch (start us, length us, event | category | flops | bytes accessed | tf_op | source)
XLA Modules:
  0.0 163.2 jit_solution(1344526380168885838)
XLA Ops:
  0.0 0.0 copy-start.2
  0.0 0.0 copy-start
  0.0 0.8 broadcast_multiply_fusion
  0.8 0.1 multiply_multiply_fusion
  0.9 0.9 multiply_bitcast_fusion
  1.7 0.3 broadcast_in_dim.9.row_y
  2.0 0.3 broadcast_in_dim.10.scale
  2.3 0.3 broadcast_in_dim.8.row_x
  2.5 0.0 copy-done.2
  2.5 0.0 copy-done
  2.5 19.0 %shard_map.55 = (bf16[8192,128]{1,0:T(8,128)(2,1)S(1)}, f32[128,128]{1,0:T(8,128)S(1)}) custom-call(s32[32,128]{1,0:T(8,128)S(1)} %bitcast.13, f32[32,128]{1,0:T(8,128)S(1)} %get-tuple-element.10.col_x, f32[32,128]{1,0:T(8,128)S(1)} %get-tuple-element.9.col_y, bf16[4096,128]{1,0:T(8,128)(2,1)S(1)} %copy-done), custom_call_target="tpu_custom_call" | custom-call | tf_op jit(solution)/shard_map/pallas_call | solution.py:97
  21.5 0.0 copy-start.1
  21.6 103.7 %shard_map.56.sketch = bf16[1536,128]{1,0:T(8,128)(2,1)S(1)} custom-call(bf16[128,64,128]{2,1,0:T(8,128)(2,1)S(1)} %bitcast.10, f32[128,1,128]{2,1,0:T(1,128)S(1)} %bitcast.12, f32[1536,128]{1,0:T(8,128)S(1)} %broadcast_in_dim.8.row_x, f32[1536,128]{1,0:T(8,128)S(1)} %broadcast_in_dim.9.row_y, f32[1536,128]{1,0:T(8,128)S(1)} %broadcast_in_dim.10.scale), custom_call_target="tpu_custom_call" | custom-call | tf_op jit(solution)/shard_map/pallas_call | solution.py:229
  125.2 0.0 copy-done.1
  125.2 37.1 %shard_map.57 = f32[1536,128]{1,0:T(8,128)S(1)} custom-call(bf16[1536,128]{1,0:T(8,128)(2,1)S(1)} %shard_map.56.sketch, bf16[4,128,128]{2,1,0:T(8,128)(2,1)S(1)} %bitcast.11), custom_call_target="tpu_custom_call" | custom-call | tf_op jit(solution)/shard_map/pallas_call | solution.py:415
  162.4 0.9 copy.7
Async XLA Ops:
  0.0 2.5 %copy-start.2 = (s32[4096,1]{0,1:T(1,128)S(1)}, s32[4096,1]{0,1:T(1,128)}, u32[]{:S(2)}) copy-start(s32[4096,1]{0,1:T(1,128)} %param.6) | copy-start | bytes 49156
  0.0 2.5 %copy-start = (bf16[4096,128]{1,0:T(8,128)(2,1)S(1)}, bf16[4096,128]{1,0:T(8,128)(2,1)}, u32[]{:S(2)}) copy-start(bf16[4096,128]{1,0:T(8,128)(2,1)} %omega.1) | copy-start | bytes 3145732
  21.5 103.7 %copy-start.1 = (bf16[1,4,128,128]{3,2,1,0:T(8,128)(2,1)S(1)}, bf16[1,4,128,128]{3,2,1,0:T(8,128)(2,1)}, u32[]{:S(2)}) copy-start(bf16[1,4,128,128]{3,2,1,0:T(8,128)(2,1)} %param.9) | copy-start | bytes 393220

commit v2 on v1

v2 whole, which is shorter than its diff:
```python
import functools
import math

import jax
import jax.numpy as jnp
from jax import lax
from jax.experimental import pallas as pl
from jax.experimental.pallas import tpu as pltpu
from jax.sharding import PartitionSpec as P

MESH = pl.DeviceIdType.MESH
SINE = (4.4415356787207045, -7.2646801556685014, 3.252047353220934)
COSINE = (1.414204078817102, -6.977641981219209, 5.715237646584958, -1.728346667500456)


def node_points(node_index, node_count):
    angles = 2.0 * math.pi / node_count * (node_index.astype(jnp.float32) + 0.5)
    radius = 1.0 + 0.25 * jnp.cos(3.0 * angles)
    return (radius * jnp.cos(angles), radius * jnp.sin(angles))


def pack_kernel(
    capacity,
    node_count,
    owners,
    columns,
    omega,
    chunks_out,
    places,
    placed,
    table,
    wide,
    plain,
    sem,
):
    blocks, lanes = owners.shape
    count, stride, _ = chunks_out.shape
    owner_at = lax.broadcasted_iota(jnp.int32, (count, lanes), 0)
    before = (
        lax.broadcasted_iota(jnp.int32, (lanes, lanes), 0)
        < lax.broadcasted_iota(jnp.int32, (lanes, lanes), 1)
    ).astype(jnp.float32)
    counted = jnp.concatenate([before, jnp.ones_like(before)], axis=1).astype(jnp.bfloat16)
    rank_at = lax.broadcasted_iota(jnp.int32, (capacity, lanes), 0)
    wide[...] = jnp.zeros_like(wide)
    table[...] = jnp.zeros_like(table)
    plain[...] = omega[...].astype(jnp.float32)

    def one_block(index, running):
        here = pl.ds(index, 1)
        owner, column = owners[here, :], columns[here, :]
        named = owner_at == owner
        onehot = named.astype(jnp.float32).astype(jnp.bfloat16)
        counts = jnp.dot(onehot, counted, preferred_element_type=jnp.float32)
        earlier = counts[:, :lanes] + running
        rank = jnp.sum(jnp.where(named, earlier, 0.0), axis=0, keepdims=True).astype(jnp.int32)
        places[here, :] = owner * stride + rank
        ranked = rank_at == rank
        digits = [
            jnp.where(ranked, digit.astype(jnp.float32), 0.0).astype(jnp.bfloat16)
            for digit in (column // 256, column % 256)
        ]
        table[...] += lax.dot_general(
            onehot,
            jnp.concatenate(digits, axis=0),
            (((1,), (1,)), ((), ())),
            preferred_element_type=jnp.float32,
        )
        return running + counts[:, lanes:]

    lax.fori_loop(0, blocks, one_block, jnp.zeros((count, lanes), jnp.float32), unroll=8)
    copy = pltpu.make_async_copy(places, placed, sem)
    copy.start()
    digits = table[...]
    column = digits[:, :capacity] * 256.0 + digits[:, capacity:]
    turn = node_count / 16.0 / (2.0 * math.pi)
    point = jnp.concatenate([v * turn for v in node_points(column, node_count)], axis=1)
    pieces = thirds(point)
    copy.wait()

    @pl.loop(0, blocks)
    def _(block):
        for first in range(0, lanes, 8):
            rows = plain[pl.ds(pl.multiple_of(block * lanes + first, 8), 8), :]
            for i in range(8):
                wide[pl.ds(placed[block, first + i], 1), :] = rows[i : i + 1]

    chunks_out[...] = wide[...].reshape(chunks_out.shape).astype(jnp.bfloat16)
    padding = jnp.zeros((count, stride - capacity - 3, lanes), jnp.float32)
    chunks_out[:, capacity:, :] = jnp.concatenate(
        [piece.astype(jnp.float32)[:, None, :] for piece in pieces] + [padding], axis=1
    ).astype(jnp.bfloat16)


def packed_chunks(omega, owners, columns, count, node_count):
    samples, width = omega.shape
    lanes = 128
    blocks = samples // lanes
    capacity = 2 * samples // count
    stride = capacity + 16
    vmem = pl.BlockSpec(memory_space=pltpu.VMEM)
    return pl.pallas_call(
        functools.partial(pack_kernel, capacity, node_count),
        out_shape=jax.ShapeDtypeStruct((count, stride, width), jnp.bfloat16),
        in_specs=[vmem] * 3,
        out_specs=vmem,
        scratch_shapes=[
            pltpu.VMEM((blocks, lanes), jnp.int32),
            pltpu.SMEM((blocks, lanes), jnp.int32),
            pltpu.VMEM((count, 2 * capacity), jnp.float32),
            pltpu.VMEM((count * stride, width), jnp.float32),
            pltpu.VMEM((samples, width), jnp.float32),
            pltpu.SemaphoreType.DMA,
        ],
        compiler_params=pltpu.CompilerParams(vmem_limit_bytes=40 << 20),
    )(owners.reshape(blocks, lanes), columns.reshape(blocks, lanes), omega)


def thirds(values):
    high = values.astype(jnp.bfloat16)
    rest = values - high.astype(jnp.float32)
    middle = rest.astype(jnp.bfloat16)
    low = (rest - middle.astype(jnp.float32)).astype(jnp.bfloat16)
    return high, middle, low


def kernel_values(x, y, col_x, col_y):
    dx = x - col_x
    dy = y - col_y
    square = jnp.maximum(dx * dx + dy * dy, 1e-30)
    turns = square * lax.rsqrt(square)
    part = turns - jnp.round(turns)
    amplitude = lax.rsqrt(turns + 0.5 / math.pi)
    z = part * part
    sine = part * (SINE[0] + z * (SINE[1] + z * SINE[2]))
    cosine = COSINE[0] + z * (COSINE[1] + z * (COSINE[2] + z * COSINE[3]))
    scaled = amplitude * sine
    return (amplitude - scaled * sine).astype(jnp.bfloat16), (scaled * cosine).astype(jnp.bfloat16)


def sketch_kernel(shape, capacity, chunks, row_x, row_y, scale, out, got, total, sent, got_sems):
    src_count, tgt_count = shape
    src, tgt = lax.axis_index("src"), lax.axis_index("tgt")
    rows, lanes = row_x.shape
    width = chunks.shape[2]
    turns = min(8, tgt_count)
    step, each = rows // turns, tgt_count // turns
    columns = tgt_count * capacity
    wrapped = lambda index, size: jnp.where(index >= size, index - size, index)

    def send(group, place):
        there = (wrapped(src + group, src_count), wrapped(tgt + place, tgt_count))
        pltpu.make_async_remote_copy(
            src_ref=chunks.at[there[0] * tgt_count + there[1]],
            dst_ref=got.at[group, place],
            send_sem=sent,
            recv_sem=got_sems.at[group],
            device_id=there,
            device_id_type=MESH,
        ).start()

    def greet(group, place):
        there = (wrapped(src + group, src_count), wrapped(tgt + place, tgt_count))
        pl.semaphore_signal(barrier, inc=1, device_id=there, device_id_type=MESH)

    barrier = pltpu.get_barrier_semaphore()

    @pl.loop(1, tgt_count)
    def _(place):
        greet(0, place)

    @pl.loop(1, src_count)
    def _(group):
        @pl.loop(0, tgt_count)
        def _(place):
            greet(group, place)

    pltpu.make_async_copy(chunks.at[src * tgt_count + tgt], got.at[0, 0], got_sems.at[0]).start()
    total[...] = jnp.zeros_like(total)
    pl.semaphore_wait(barrier, src_count * tgt_count - 1)

    @pl.loop(1, tgt_count)
    def _(place):
        send(0, place)

    def one_group(group, more):
        pltpu.make_async_copy(got.at[group], got.at[group], got_sems.at[group]).wait()
        pieces = got[group, :, capacity:, :].astype(jnp.float32)
        points = (pieces[:, 2] + pieces[:, 1]) + pieces[:, 0]
        join = lambda i, at: jnp.concatenate(
            [points[i : i + 1, at : at + capacity], points[i + 1 : i + 2, at : at + capacity]], axis=1
        )
        col_x = [join(i, 0) for i in range(0, tgt_count, 2)]
        col_y = [join(i, capacity) for i in range(0, tgt_count, 2)]
        weights = got[group, :, :capacity, :].reshape(columns, width)

        @pl.loop(0, rows // step)
        def _(index):
            if more:
                for i in range(each):
                    send(group + 1, index * each + i)
            here = pl.ds(pl.multiple_of(index * step, step), step)
            x, y = row_x[here, :], row_y[here, :]
            values = [kernel_values(x, y, a, b) for a, b in zip(col_x, col_y)]
            parts = jnp.concatenate(
                [jnp.concatenate([v[k] for v in values], axis=1) for k in (0, 1)], axis=0
            )
            both = jnp.dot(parts, weights, preferred_element_type=jnp.float32)
            crossed = both[step:]
            half = width // 2
            total[here, :] += both[:step] + jnp.concatenate(
                [-crossed[:, half:], crossed[:, :half]], axis=1
            )

    @pl.loop(0, src_count - 1)
    def _(group):
        one_group(group, True)

    one_group(src_count - 1, False)
    out[...] = (total[...] * scale[...]).astype(jnp.bfloat16)
    rest = chunks.at[pl.ds(0, src_count * tgt_count - 1)]
    pltpu.make_async_copy(rest, rest, sent).wait()


def sketch_rows(row_first, impedance_rows, chunks, mesh_shape, node_count):
    rows = impedance_rows.shape[0]
    count, stride, width = chunks.shape
    turn = node_count / 16.0 / (2.0 * math.pi)
    row_x, row_y = node_points(row_first + jnp.arange(rows, dtype=jnp.int32), node_count)
    spread = lambda v: jnp.broadcast_to(v[:, None], (rows, 128))
    vmem = pl.BlockSpec(memory_space=pltpu.VMEM)
    return pl.pallas_call(
        functools.partial(sketch_kernel, mesh_shape, stride - 16),
        out_shape=jax.ShapeDtypeStruct((rows, width), jnp.bfloat16),
        in_specs=[vmem] * 4,
        out_specs=vmem,
        scratch_shapes=[
            pltpu.VMEM((*mesh_shape, stride, width), jnp.bfloat16),
            pltpu.VMEM((rows, width), jnp.float32),
            pltpu.SemaphoreType.DMA,
            pltpu.SemaphoreType.DMA((mesh_shape[0],)),
        ],
        compiler_params=pltpu.CompilerParams(
            collective_id=1, has_side_effects=True, vmem_limit_bytes=48 << 20
        ),
    )(
        chunks,
        spread(row_x * turn),
        spread(row_y * turn),
        spread(impedance_rows / math.sqrt(2.0 * math.pi)),
    )


def split(values, axis, order):
    high = values.astype(jnp.bfloat16)
    rest = values - high.astype(jnp.float32)
    middle = rest.astype(jnp.bfloat16)
    low = (rest - middle.astype(jnp.float32)).astype(jnp.bfloat16)
    pieces = (high, middle, low)
    return jnp.concatenate([pieces[i] for i in order], axis=axis)


LEFT, RIGHT = (0, 0, 1, 0, 1, 2), (0, 1, 0, 2, 1, 0)


def product(first, second, first_axis=1, second_axis=0):
    return lax.dot_general(
        split(first, first_axis, LEFT),
        split(second, second_axis, RIGHT),
        (((first_axis,), (second_axis,)), ((), ())),
        preferred_element_type=jnp.float32,
    )


def spread_rows(row, count):
    return jnp.broadcast_to(row, (count, row.shape[1]))


def eliminate_panel(panel, first, lanes):
    pieces = panel.shape[0] // 8
    rows = [panel[8 * i : 8 * i + 8] for i in range(pieces)]
    sublane = lax.broadcasted_iota(jnp.int32, (8, lanes), 0)
    twice = lambda v: jnp.concatenate([v, v], axis=1)
    done = []
    for top in range(pieces):
        columns = [
            [
                jnp.take_along_axis(
                    rows[i][:, :lanes],
                    jnp.full((8, lanes), first + 8 * top + t, jnp.int32),
                    axis=1,
                )
                for i in range(top, pieces)
            ]
            for t in range(8)
        ]
        for t in range(8):
            pivot = spread_rows(columns[t][0][t : t + 1], 8)
            inverse = 1.0 / pivot
            row = rows[top][t : t + 1]
            done.append(row * twice(lax.rsqrt(pivot[0:1])))
            factors = [c * inverse for c in columns[t]]
            factors[0] = jnp.where(sublane > t, factors[0], 0.0)
            for u in range(t + 1, 8):
                entry = spread_rows(columns[u][0][t : t + 1], 8)
                columns[u] = [c - f * entry for c, f in zip(columns[u], factors)]
            full_row = spread_rows(row, 8)
            for i, f in enumerate(factors):
                rows[top + i] = rows[top + i] - twice(f) * full_row
    return jnp.concatenate(done, axis=0)


def factor_solve(gram_matrix, right):
    size, block = gram_matrix.shape[0], 32
    diagonal = lax.broadcasted_iota(jnp.int32, (size, size), 0) == lax.broadcasted_iota(
        jnp.int32, (size, size), 1
    )
    trace = jnp.sum(jnp.where(diagonal, gram_matrix, 0.0), axis=(0, 1), keepdims=True)
    shifted = gram_matrix + jnp.where(diagonal, 0.25 * trace / size + 1e-06, 0.0)
    rest = jnp.concatenate([shifted, right], axis=1)
    solved = []
    for first in range(0, size, block):
        panel = eliminate_panel(rest[:block], first, size)
        solved.append(panel[:, size:])
        if first + block < size:
            rest = rest[block:] - product(panel[:, :size], panel, 0, 0)[first + block :]
    return jnp.concatenate(solved, axis=0)


def merge_kernel(rows, sketch, maps, out, sends, gots, send_sems, got_sems):
    src, tgt = lax.axis_index("src"), lax.axis_index("tgt")
    mates = (
        tgt + 1 - 2 * (tgt % 2),
        tgt + 2 - 4 * ((tgt // 2) % 2),
        tgt + 3 - 2 * (tgt % 4),
        tgt + 4 - 8 * ((tgt // 4) % 2),
    )
    barrier = pltpu.get_barrier_semaphore()
    for mate in mates:
        pl.semaphore_signal(barrier, inc=1, device_id=(src, mate), device_id_type=MESH)
    pl.semaphore_wait(barrier, len(mates))

    copies = []

    def post(values, targets):
        source = sends.at[sum(len(c) > 0 for c in copies)]
        source[...] = values
        base = sum(len(c) for c in copies)
        batch = []
        for i, target in enumerate(targets):
            copy = pltpu.make_async_remote_copy(
                src_ref=source,
                dst_ref=gots.at[base + i],
                send_sem=send_sems.at[base + i],
                recv_sem=got_sems.at[base + i],
                device_id=(src, mates[target]),
                device_id_type=MESH,
            )
            copy.start()
            batch.append((copy, base + i))
        copies.append(batch)
        return batch

    def take(batch):
        values = []
        for copy, slot in batch:
            copy.wait_recv()
            values.append(gots[slot])
        return values

    cross = lax.dot_general(
        sketch[...], sketch[...], (((0,), (0,)), ((), ())), preferred_element_type=jnp.float32
    )
    wide_maps = [maps[k].astype(jnp.float32) for k in range(4)]
    images = [product(cross, m) for m in wide_maps]
    gram_matrix = product(wide_maps[0], images[0], 0, 0) / rows
    turned = factor_solve(gram_matrix, wide_maps[0].T)
    for level in range(3):
        part = product(turned, images[level + 1]) / (rows * 2**level)
        if level == 0:
            batch = post(part, (0,))
            own = part
        else:
            batch = post(part, (0, 1, 2))
            near, far, beyond = take(batch)
            own = part + near
            if level == 1:
                other = far + beyond
            else:
                own = own + (far + beyond)
                batch = post(own, (3,))
        mine = product(own, own, 0, 0)
        right = product(own, turned, 0, 0)
        if level != 1:
            (other,) = take(batch)
        gram_matrix = (mine + product(other, other, 0, 0)) / 2.0
        turned = factor_solve(gram_matrix, right)
    for batch in copies:
        for copy, _ in batch:
            copy.wait_send()
    turned = split(turned, 1, (0, 1, 2))
    sketch_here = sketch[...]
    out[...] = lax.dot_general(
        jnp.concatenate([sketch_here] * 3, axis=1),
        turned,
        (((1,), (1,)), ((), ())),
        preferred_element_type=jnp.float32,
    )


def merged_bases(sketch, maps_here):
    rows, width = sketch.shape
    tile = (width, width)
    return pl.pallas_call(
        functools.partial(merge_kernel, rows),
        out_shape=jax.ShapeDtypeStruct((rows, width), jnp.float32),
        in_specs=[pl.BlockSpec(memory_space=pltpu.VMEM)] * 2,
        out_specs=pl.BlockSpec(memory_space=pltpu.VMEM),
        scratch_shapes=[
            pltpu.VMEM((4, *tile), jnp.float32),
            pltpu.VMEM((8, *tile), jnp.float32),
            pltpu.SemaphoreType.DMA((8,)),
            pltpu.SemaphoreType.DMA((8,)),
        ],
        compiler_params=pltpu.CompilerParams(
            collective_id=0, has_side_effects=True, vmem_limit_bytes=40 << 20
        ),
    )(sketch, maps_here)


def sketch_of(omega, owners, columns, impedance):
    mesh_shape = (lax.axis_size("src"), lax.axis_size("tgt"))
    rows = impedance.shape[0]
    node_count = mesh_shape[1] * rows
    chunks = packed_chunks(omega, owners, columns, mesh_shape[0] * mesh_shape[1], node_count)
    first = lax.axis_index("tgt") * rows
    return sketch_rows(first, impedance, chunks, mesh_shape, node_count)


def per_device(omega, owners, columns, impedance, level_maps):
    return merged_bases(sketch_of(omega, owners, columns, impedance), level_maps[0])[None]


def solution(mesh):
    in_specs = (
        P(("src", "tgt"), None),
        P(("src", "tgt"), None),
        P(("src", "tgt")),
        P("tgt"),
        P("src", None, None, None),
    )
    out_specs = P("src", "tgt", None)
    return jax.shard_map(
        per_device, mesh=mesh, in_specs=in_specs, out_specs=out_specs, check_vma=False
    )
```

time: 163 us -> 152 us (0.933)
  Pallas kernels: 160 us -> 147 us
    pallas_call x2, Pallas kernels: 123 us -> 111 us  [the longest x1 103 us: sketch_rows(): pl.pallas_call(functools.partial(sketch_kernel, mesh_shape, stride - 16),...]
where the time goes in v2:
time: 152 us; the launch traced here: 151 us
  Pallas kernels  147 us (97%)
  local copies, waits for them, and re-layouts  3.1 us (2%)
    pallas_call x1, Pallas kernels, sketch_rows(): pl.pallas_call(functools.partial(sketch_kernel, mesh_shape, stride - 16),...  103 us
    pallas_call x1, Pallas kernels, merged_bases(): pl.pallas_call(functools.partial(merge_kernel, rows), out_shape=jax.Shape...  36.1 us
    pallas_call x1, Pallas kernels, packed_chunks(): pl.pallas_call(functools.partial(pack_kernel, capacity, node_count), out_...  7.19 us

profile of v2, /device:TPU:10, one launch (start us, length us, event | category | flops | bytes accessed | tf_op | source)
XLA Modules:
  0.0 150.7 jit_solution(8311550272945869387)
XLA Ops:
  0.0 0.0 copy-start
  0.0 0.8 broadcast_multiply_fusion
  0.8 0.1 multiply_multiply_fusion
  0.9 0.3 broadcast_in_dim.9.row_y
  1.1 0.3 broadcast_in_dim.10.scale
  1.4 0.3 broadcast_in_dim.8.row_x
  1.7 0.0 copy-done
  1.7 0.0 copy-start.2
  1.7 0.7 copy-done.2
  2.4 0.0 copy-start.3
  2.4 0.7 copy-done.3
  3.1 7.2 %shard_map.55.chunks = bf16[128,80,128]{2,1,0:T(8,128)(2,1)S(1)} custom-call(s32[32,128]{1,0:T(8,128)S(1)} %bitcast.6, s32[32,128]{1,0:T(8,128)S(1)} %bitcast.7, bf16[4096,128]{1,0:T(8,128)(2,1)S(1)} %copy-done), custom_call_target="tpu_custom_call" | custom-call | tf_op jit(solution)/shard_map/pallas_call | solution.py:102
  10.3 0.0 copy-start.1
  10.3 103.4 %shard_map.56.sketch = bf16[1536,128]{1,0:T(8,128)(2,1)S(1)} custom-call(bf16[128,80,128]{2,1,0:T(8,128)(2,1)S(1)} %shard_map.55.chunks, f32[1536,128]{1,0:T(8,128)S(1)} %broadcast_in_dim.8.row_x, f32[1536,128]{1,0:T(8,128)S(1)} %broadcast_in_dim.9.row_y, f32[1536,128]{1,0:T(8,128)S(1)} %broadcast_in_dim.10.scale), custom_call_target="tpu_custom_call" | custom-call | tf_op jit(solution)/shard_map/pallas_call | solution.py:232
  113.7 0.0 copy-done.1
  113.7 36.1 %shard_map.57 = f32[1536,128]{1,0:T(8,128)S(1)} custom-call(bf16[1536,128]{1,0:T(8,128)(2,1)S(1)} %shard_map.56.sketch, bf16[4,128,128]{2,1,0:T(8,128)(2,1)S(1)} %bitcast.5), custom_call_target="tpu_custom_call" | custom-call | tf_op jit(solution)/shard_map/pallas_call | solution.py:414
  149.8 0.9 copy.7
Async XLA Ops:
  0.0 1.7 %copy-start = (bf16[4096,128]{1,0:T(8,128)(2,1)S(1)}, bf16[4096,128]{1,0:T(8,128)(2,1)}, u32[]{:S(2)}) copy-start(bf16[4096,128]{1,0:T(8,128)(2,1)} %omega.1) | copy-start | bytes 3145732
  1.7 0.7 copy-start.2
  2.4 0.7 copy-start.3
  10.3 103.4 %copy-start.1 = (bf16[1,4,128,128]{3,2,1,0:T(8,128)(2,1)S(1)}, bf16[1,4,128,128]{3,2,1,0:T(8,128)(2,1)}, u32[]{:S(2)}) copy-start(bf16[1,4,128,128]{3,2,1,0:T(8,128)(2,1)} %param.9) | copy-start | bytes 393220

commit v3 on v2

--- a/solution.py
+++ b/solution.py
@@ -26,6 +26,7 @@
     columns,
     omega,
     chunks_out,
+    points_out,
     places,
     placed,
     table,
@@ -34,7 +35,7 @@
     sem,
 ):
     blocks, lanes = owners.shape
-    count, stride, _ = chunks_out.shape
+    count = points_out.shape[0]
     owner_at = lax.broadcasted_iota(jnp.int32, (count, lanes), 0)
     before = (
         lax.broadcasted_iota(jnp.int32, (lanes, lanes), 0)
@@ -54,7 +55,7 @@
         counts = jnp.dot(onehot, counted, preferred_element_type=jnp.float32)
         earlier = counts[:, :lanes] + running
         rank = jnp.sum(jnp.where(named, earlier, 0.0), axis=0, keepdims=True).astype(jnp.int32)
-        places[here, :] = owner * stride + rank
+        places[here, :] = owner * capacity + rank
         ranked = rank_at == rank
         digits = [
             jnp.where(ranked, digit.astype(jnp.float32), 0.0).astype(jnp.bfloat16)
@@ -74,8 +75,8 @@
     digits = table[...]
     column = digits[:, :capacity] * 256.0 + digits[:, capacity:]
     turn = node_count / 16.0 / (2.0 * math.pi)
-    point = jnp.concatenate([v * turn for v in node_points(column, node_count)], axis=1)
-    pieces = thirds(point)
+    point_x, point_y = node_points(column, node_count)
+    points_out[...] = jnp.concatenate(gridded((point_x * turn, point_y * turn), 0.5), axis=1)
     copy.wait()
 
     @pl.loop(0, blocks)
@@ -85,11 +86,7 @@
             for i in range(8):
                 wide[pl.ds(placed[block, first + i], 1), :] = rows[i : i + 1]
 
-    chunks_out[...] = wide[...].reshape(chunks_out.shape).astype(jnp.bfloat16)
-    padding = jnp.zeros((count, stride - capacity - 3, lanes), jnp.float32)
-    chunks_out[:, capacity:, :] = jnp.concatenate(
-        [piece.astype(jnp.float32)[:, None, :] for piece in pieces] + [padding], axis=1
-    ).astype(jnp.bfloat16)
+    chunks_out[...] = wide[...].astype(jnp.bfloat16)
 
 
 def packed_chunks(omega, owners, columns, count, node_count):
@@ -97,18 +94,20 @@
     lanes = 128
     blocks = samples // lanes
     capacity = 2 * samples // count
-    stride = capacity + 16
     vmem = pl.BlockSpec(memory_space=pltpu.VMEM)
     return pl.pallas_call(
         functools.partial(pack_kernel, capacity, node_count),
-        out_shape=jax.ShapeDtypeStruct((count, stride, width), jnp.bfloat16),
+        out_shape=(
+            jax.ShapeDtypeStruct((count * capacity, width), jnp.bfloat16),
+            jax.ShapeDtypeStruct((count, 2 * capacity), jnp.float32),
+        ),
         in_specs=[vmem] * 3,
-        out_specs=vmem,
+        out_specs=(vmem, vmem),
         scratch_shapes=[
             pltpu.VMEM((blocks, lanes), jnp.int32),
             pltpu.SMEM((blocks, lanes), jnp.int32),
             pltpu.VMEM((count, 2 * capacity), jnp.float32),
-            pltpu.VMEM((count * stride, width), jnp.float32),
+            pltpu.VMEM((count * capacity, width), jnp.float32),
             pltpu.VMEM((samples, width), jnp.float32),
             pltpu.SemaphoreType.DMA,
         ],
@@ -116,18 +115,15 @@
     )(owners.reshape(blocks, lanes), columns.reshape(blocks, lanes), omega)
 
 
-def thirds(values):
-    high = values.astype(jnp.bfloat16)
-    rest = values - high.astype(jnp.float32)
-    middle = rest.astype(jnp.bfloat16)
-    low = (rest - middle.astype(jnp.float32)).astype(jnp.bfloat16)
-    return high, middle, low
+def gridded(points, shift):
+    x, y = points
+    return (jnp.floor(x * 16384.0 + (0.5 - shift)) + shift) / 16384.0, y
 
 
 def kernel_values(x, y, col_x, col_y):
     dx = x - col_x
     dy = y - col_y
-    square = jnp.maximum(dx * dx + dy * dy, 1e-30)
+    square = dx * dx + dy * dy
     turns = square * lax.rsqrt(square)
     part = turns - jnp.round(turns)
     amplitude = lax.rsqrt(turns + 0.5 / math.pi)
@@ -138,67 +134,80 @@
     return (amplitude - scaled * sine).astype(jnp.bfloat16), (scaled * cosine).astype(jnp.bfloat16)
 
 
-def sketch_kernel(shape, capacity, chunks, row_x, row_y, scale, out, got, total, sent, got_sems):
-    src_count, tgt_count = shape
+def sketch_kernel(
+    sides, lead, chunks, points, row_x, row_y, scale, out, got, got_points, total, sent, got_sems
+):
     src, tgt = lax.axis_index("src"), lax.axis_index("tgt")
     rows, lanes = row_x.shape
-    width = chunks.shape[2]
-    turns = min(8, tgt_count)
-    step, each = rows // turns, tgt_count // turns
-    columns = tgt_count * capacity
-    wrapped = lambda index, size: jnp.where(index >= size, index - size, index)
+    count, capacity, width = chunks.shape
+    groups, places = got.shape[:2]
+    side_x, side_y, side_z = sides
+    columns = places * capacity
+    step, each = rows // 2, places // 2
+    me = (src // 2, src % 2, tgt // side_z, tgt % side_z)
+
+    def wrapped(index, size):
+        return jnp.where(index >= size, index - size, index)
+
+    def there(group, place):
+        dx, dy, dz = place // side_y, place % side_y, group // 2
+        for back in (dx, dy):
+            dz = jnp.where(dz < back, dz + side_z - back, dz - back)
+        core = wrapped(me[1] + group % 2, 2)
+        return (
+            2 * wrapped(me[0] + dx, side_x) + core,
+            side_z * wrapped(me[2] + dy, side_y) + wrapped(me[3] + dz, side_z),
+        )
+
+    def each_other(first, last, act):
+        for group in range(first, last):
+            @pl.loop(1 if group == 0 else 0, places)
+            def _(place):
+                act(group, place)
+
+    def greet(group, place):
+        pl.semaphore_signal(barrier, inc=1, device_id=there(group, place), device_id_type=MESH)
 
     def send(group, place):
-        there = (wrapped(src + group, src_count), wrapped(tgt + place, tgt_count))
-        pltpu.make_async_remote_copy(
-            src_ref=chunks.at[there[0] * tgt_count + there[1]],
-            dst_ref=got.at[group, place],
-            send_sem=sent,
-            recv_sem=got_sems.at[group],
-            device_id=there,
-            device_id_type=MESH,
-        ).start()
-
-    def greet(group, place):
-        there = (wrapped(src + group, src_count), wrapped(tgt + place, tgt_count))
-        pl.semaphore_signal(barrier, inc=1, device_id=there, device_id_type=MESH)
+        target = there(group, place)
+        owner = target[0] * side_y * side_z + target[1]
+        for kind, (source, landing) in enumerate(((points, got_points), (chunks, got))):
+            pltpu.make_async_remote_copy(
+                src_ref=source.at[owner],
+                dst_ref=landing.at[group, place],
+                send_sem=sent.at[kind],
+                recv_sem=got_sems.at[kind, group],
+                device_id=target,
+                device_id_type=MESH,
+            ).start()
 
     barrier = pltpu.get_barrier_semaphore()
-
-    @pl.loop(1, tgt_count)
-    def _(place):
-        greet(0, place)
-
-    @pl.loop(1, src_count)
-    def _(group):
-        @pl.loop(0, tgt_count)
-        def _(place):
-            greet(group, place)
-
-    pltpu.make_async_copy(chunks.at[src * tgt_count + tgt], got.at[0, 0], got_sems.at[0]).start()
+    each_other(0, groups, greet)
+    own = src * side_y * side_z + tgt
+    pltpu.make_async_copy(points.at[own], got_points.at[0, 0], got_sems.at[0, 0]).start()
+    pltpu.make_async_copy(chunks.at[own], got.at[0, 0], got_sems.at[1, 0]).start()
     total[...] = jnp.zeros_like(total)
-    pl.semaphore_wait(barrier, src_count * tgt_count - 1)
-
-    @pl.loop(1, tgt_count)
-    def _(place):
-        send(0, place)
+    pl.semaphore_wait(barrier, count - 1)
+    each_other(0, lead, send)
 
     def one_group(group, more):
-        pltpu.make_async_copy(got.at[group], got.at[group], got_sems.at[group]).wait()
-        pieces = got[group, :, capacity:, :].astype(jnp.float32)
-        points = (pieces[:, 2] + pieces[:, 1]) + pieces[:, 0]
+        for kind, landing in enumerate((got_points, got)):
+            pltpu.make_async_copy(
+                landing.at[group], landing.at[group], got_sems.at[kind, group]
+            ).wait()
+        pairs = got_points[group].reshape(places, 2 * capacity)
         join = lambda i, at: jnp.concatenate(
-            [points[i : i + 1, at : at + capacity], points[i + 1 : i + 2, at : at + capacity]], axis=1
+            [pairs[i : i + 1, at : at + capacity], pairs[i + 1 : i + 2, at : at + capacity]], axis=1
         )
-        col_x = [join(i, 0) for i in range(0, tgt_count, 2)]
-        col_y = [join(i, capacity) for i in range(0, tgt_count, 2)]
-        weights = got[group, :, :capacity, :].reshape(columns, width)
+        col_x = [join(i, 0) for i in range(0, places, 2)]
+        col_y = [join(i, capacity) for i in range(0, places, 2)]
+        weights = got[group].reshape(columns, width)
 
         @pl.loop(0, rows // step)
         def _(index):
             if more:
                 for i in range(each):
-                    send(group + 1, index * each + i)
+                    send(group + lead, index * each + i)
             here = pl.ds(pl.multiple_of(index * step, step), step)
             x, y = row_x[here, :], row_y[here, :]
             values = [kernel_values(x, y, a, b) for a, b in zip(col_x, col_y)]
@@ -212,41 +221,49 @@
                 [-crossed[:, half:], crossed[:, :half]], axis=1
             )
 
-    @pl.loop(0, src_count - 1)
+    @pl.loop(0, groups - lead)
     def _(group):
         one_group(group, True)
 
-    one_group(src_count - 1, False)
+    @pl.loop(groups - lead, groups)
+    def _(group):
+        one_group(group, False)
+
     out[...] = (total[...] * scale[...]).astype(jnp.bfloat16)
-    rest = chunks.at[pl.ds(0, src_count * tgt_count - 1)]
-    pltpu.make_async_copy(rest, rest, sent).wait()
-
-
-def sketch_rows(row_first, impedance_rows, chunks, mesh_shape, node_count):
+    for kind, source in enumerate((points, chunks)):
+        rest = source.at[pl.ds(0, count - 1)]
+        pltpu.make_async_copy(rest, rest, sent.at[kind]).wait()
+
+
+def sketch_rows(row_first, impedance_rows, chunks, points, mesh_shape, node_count):
     rows = impedance_rows.shape[0]
-    count, stride, width = chunks.shape
+    count, capacity, width = chunks.shape
+    side = math.isqrt(mesh_shape[1])
+    sides = (mesh_shape[0] // 2, side, side)
+    landing = (2 * side, count // (2 * side))
     turn = node_count / 16.0 / (2.0 * math.pi)
     row_x, row_y = node_points(row_first + jnp.arange(rows, dtype=jnp.int32), node_count)
     spread = lambda v: jnp.broadcast_to(v[:, None], (rows, 128))
     vmem = pl.BlockSpec(memory_space=pltpu.VMEM)
     return pl.pallas_call(
-        functools.partial(sketch_kernel, mesh_shape, stride - 16),
+        functools.partial(sketch_kernel, sides, 3),
         out_shape=jax.ShapeDtypeStruct((rows, width), jnp.bfloat16),
-        in_specs=[vmem] * 4,
+        in_specs=[vmem] * 5,
         out_specs=vmem,
         scratch_shapes=[
-            pltpu.VMEM((*mesh_shape, stride, width), jnp.bfloat16),
+            pltpu.VMEM((*landing, capacity, width), jnp.bfloat16),
+            pltpu.VMEM((*landing, 1, 2 * capacity), jnp.float32),
             pltpu.VMEM((rows, width), jnp.float32),
-            pltpu.SemaphoreType.DMA,
-            pltpu.SemaphoreType.DMA((mesh_shape[0],)),
+            pltpu.SemaphoreType.DMA((2,)),
+            pltpu.SemaphoreType.DMA((2, landing[0])),
         ],
         compiler_params=pltpu.CompilerParams(
             collective_id=1, has_side_effects=True, vmem_limit_bytes=48 << 20
         ),
     )(
         chunks,
-        spread(row_x * turn),
-        spread(row_y * turn),
+        points,
+        *(spread(v) for v in gridded((row_x * turn, row_y * turn), 0.0)),
         spread(impedance_rows / math.sqrt(2.0 * math.pi)),
     )
 
@@ -338,8 +355,6 @@
     barrier = pltpu.get_barrier_semaphore()
     for mate in mates:
         pl.semaphore_signal(barrier, inc=1, device_id=(src, mate), device_id_type=MESH)
-    pl.semaphore_wait(barrier, len(mates))
-
     copies = []
 
     def post(values, targets):
@@ -375,6 +390,7 @@
     images = [product(cross, m) for m in wide_maps]
     gram_matrix = product(wide_maps[0], images[0], 0, 0) / rows
     turned = factor_solve(gram_matrix, wide_maps[0].T)
+    pl.semaphore_wait(barrier, len(mates))
     for level in range(3):
         part = product(turned, images[level + 1]) / (rows * 2**level)
         if level == 0:
@@ -432,9 +448,12 @@
     mesh_shape = (lax.axis_size("src"), lax.axis_size("tgt"))
     rows = impedance.shape[0]
     node_count = mesh_shape[1] * rows
-    chunks = packed_chunks(omega, owners, columns, mesh_shape[0] * mesh_shape[1], node_count)
+    count = mesh_shape[0] * mesh_shape[1]
+    chunks, points = packed_chunks(omega, owners, columns, count, node_count)
+    chunks = chunks.reshape(count, -1, chunks.shape[1])
+    points = points.reshape(count, 1, -1)
     first = lax.axis_index("tgt") * rows
-    return sketch_rows(first, impedance, chunks, mesh_shape, node_count)
+    return sketch_rows(first, impedance, chunks, points, mesh_shape, node_count)
 
 
 def per_device(omega, owners, columns, impedance, level_maps):

time: 152 us -> 115 us (0.76)
  Pallas kernels: 147 us -> 110 us
    pallas_call x1, Pallas kernels: 103 us -> 69.8 us  [sketch_rows(): pl.pallas_call(functools.partial(sketch_kernel, sides, 3), out_shape=jax....]
    pallas_call x1, Pallas kernels: 36.1 us -> 33.3 us  [merged_bases(): pl.pallas_call(functools.partial(merge_kernel, rows), out_shape=jax.Shape...]
where the time goes in v3:
time: 115 us; the launch traced here: 113 us
  Pallas kernels  110 us (96%)
  local copies, waits for them, and re-layouts  1.68 us (1%)
    pallas_call x1, Pallas kernels, sketch_rows(): pl.pallas_call(functools.partial(sketch_kernel, sides, 3), out_shape=jax....  69.8 us
    pallas_call x1, Pallas kernels, merged_bases(): pl.pallas_call(functools.partial(merge_kernel, rows), out_shape=jax.Shape...  33.3 us
    pallas_call x1, Pallas kernels, packed_chunks(): pl.pallas_call(functools.partial(pack_kernel, capacity, node_count), out_...  7.04 us

profile of v3, /device:TPU:10, one launch (start us, length us, event | category | flops | bytes accessed | tf_op | source)
XLA Modules:
  0.0 112.8 jit_solution(13151476823727614731)
XLA Ops:
  0.0 0.0 copy-start.3
  0.0 0.0 copy-start.2
  0.0 0.0 copy-start
  0.0 0.8 broadcast_multiply_fusion
  0.8 0.1 multiply_multiply_fusion
  0.9 0.3 broadcast_in_dim.9.row_y
  1.2 0.3 broadcast_in_dim.10.scale
  1.4 0.3 broadcast_in_dim.8.row_x
  1.7 0.0 copy-done.3
  1.7 0.0 copy-done.2
  1.7 0.0 copy-done
  1.7 7.0 %shard_map.55 = (bf16[8192,128]{1,0:T(8,128)(2,1)S(1)}, f32[128,128]{1,0:T(8,128)S(1)}) custom-call(s32[32,128]{1,0:T(8,128)S(1)} %bitcast.10, s32[32,128]{1,0:T(8,128)S(1)} %bitcast.11, bf16[4096,128]{1,0:T(8,128)(2,1)S(1)} %copy-done), custom_call_target="tpu_custom_call" | custom-call | tf_op jit(solution)/shard_map/pallas_call | solution.py:98
  8.8 0.0 copy-start.1
  8.8 69.8 %shard_map.56.sketch = bf16[1536,128]{1,0:T(8,128)(2,1)S(1)} custom-call(bf16[128,64,128]{2,1,0:T(8,128)(2,1)S(1)} %bitcast.7, f32[128,1,128]{2,1,0:T(1,128)S(1)} %bitcast.9, f32[1536,128]{1,0:T(8,128)S(1)} %broadcast_in_dim.8.row_x, f32[1536,128]{1,0:T(8,128)S(1)} %broadcast_in_dim.9.row_y, f32[1536,128]{1,0:T(8,128)S(1)} %broadcast_in_dim.10.scale), custom_call_target="tpu_custom_call" | custom-call | tf_op jit(solution)/shard_map/pallas_call | solution.py:248
  78.6 0.0 copy-done.1
  78.6 33.3 %shard_map.57 = f32[1536,128]{1,0:T(8,128)S(1)} custom-call(bf16[1536,128]{1,0:T(8,128)(2,1)S(1)} %shard_map.56.sketch, bf16[4,128,128]{2,1,0:T(8,128)(2,1)S(1)} %bitcast.8), custom_call_target="tpu_custom_call" | custom-call | tf_op jit(solution)/shard_map/pallas_call | solution.py:430
  111.9 0.9 copy.7
Async XLA Ops:
  0.0 1.7 %copy-start.3 = (s32[4096]{0:T(1024)S(1)}, s32[4096]{0:T(1024)}, u32[]{:S(2)}) copy-start(s32[4096]{0:T(1024)} %param.7) | copy-start | bytes 49156
  0.0 1.7 %copy-start.2 = (s32[4096,1]{0,1:T(1,128)S(1)}, s32[4096,1]{0,1:T(1,128)}, u32[]{:S(2)}) copy-start(s32[4096,1]{0,1:T(1,128)} %param.6) | copy-start | bytes 49156
  0.0 1.7 %copy-start = (bf16[4096,128]{1,0:T(8,128)(2,1)S(1)}, bf16[4096,128]{1,0:T(8,128)(2,1)}, u32[]{:S(2)}) copy-start(bf16[4096,128]{1,0:T(8,128)(2,1)} %omega.1) | copy-start | bytes 3145732
  8.8 69.8 %copy-start.1 = (bf16[1,4,128,128]{3,2,1,0:T(8,128)(2,1)S(1)}, bf16[1,4,128,128]{3,2,1,0:T(8,128)(2,1)}, u32[]{:S(2)}) copy-start(bf16[1,4,128,128]{3,2,1,0:T(8,128)(2,1)} %param.9) | copy-start | bytes 393220

commit v4 on v3

--- a/solution.py
+++ b/solution.py
@@ -129,21 +129,32 @@
     amplitude = lax.rsqrt(turns + 0.5 / math.pi)
     z = part * part
     sine = part * (SINE[0] + z * (SINE[1] + z * SINE[2]))
-    cosine = COSINE[0] + z * (COSINE[1] + z * (COSINE[2] + z * COSINE[3]))
+    cosine = COSINE[0] / COSINE[3] + z * (COSINE[1] / COSINE[3] + z * (COSINE[2] / COSINE[3] + z))
     scaled = amplitude * sine
     return (amplitude - scaled * sine).astype(jnp.bfloat16), (scaled * cosine).astype(jnp.bfloat16)
 
 
 def sketch_kernel(
-    sides, lead, chunks, points, row_x, row_y, scale, out, got, got_points, total, sent, got_sems
+    sides,
+    lead,
+    chunks,
+    points,
+    row_table,
+    out,
+    got,
+    got_points,
+    row_values,
+    total,
+    sent,
+    got_sems,
 ):
     src, tgt = lax.axis_index("src"), lax.axis_index("tgt")
-    rows, lanes = row_x.shape
+    rows, lanes = total.shape[1:]
     count, capacity, width = chunks.shape
     groups, places = got.shape[:2]
     side_x, side_y, side_z = sides
     columns = places * capacity
-    step, each = rows // 2, places // 2
+    blocks = rows // lanes
     me = (src // 2, src % 2, tgt // side_z, tgt % side_z)
 
     def wrapped(index, size):
@@ -189,6 +200,13 @@
     total[...] = jnp.zeros_like(total)
     pl.semaphore_wait(barrier, count - 1)
     each_other(0, lead, send)
+    turned = row_table[...].T
+    for kind in range(3):
+        for block in range(blocks):
+            at = jnp.full((lanes, lanes), kind * blocks + block, jnp.int32)
+            row_values[kind, block * lanes : (block + 1) * lanes, :] = jnp.take_along_axis(
+                turned, at, axis=1
+            )
 
     def one_group(group, more):
         for kind, landing in enumerate((got_points, got)):
@@ -203,23 +221,18 @@
         col_y = [join(i, capacity) for i in range(0, places, 2)]
         weights = got[group].reshape(columns, width)
 
-        @pl.loop(0, rows // step)
-        def _(index):
-            if more:
-                for i in range(each):
-                    send(group + lead, index * each + i)
-            here = pl.ds(pl.multiple_of(index * step, step), step)
-            x, y = row_x[here, :], row_y[here, :]
-            values = [kernel_values(x, y, a, b) for a, b in zip(col_x, col_y)]
-            parts = jnp.concatenate(
-                [jnp.concatenate([v[k] for v in values], axis=1) for k in (0, 1)], axis=0
-            )
-            both = jnp.dot(parts, weights, preferred_element_type=jnp.float32)
-            crossed = both[step:]
-            half = width // 2
-            total[here, :] += both[:step] + jnp.concatenate(
-                [-crossed[:, half:], crossed[:, :half]], axis=1
-            )
+        if more:
+            @pl.loop(0, places)
+            def _(place):
+                send(group + lead, place)
+        x, y = row_values[0], row_values[1]
+        values = [kernel_values(x, y, a, b) for a, b in zip(col_x, col_y)]
+        parts = jnp.concatenate(
+            [jnp.concatenate([v[k] for v in values], axis=1) for k in (0, 1)], axis=0
+        )
+        both = jnp.dot(parts, weights, preferred_element_type=jnp.float32)
+        total[0] += both[:rows]
+        total[1] += both[rows:]
 
     @pl.loop(0, groups - lead)
     def _(group):
@@ -229,7 +242,10 @@
     def _(group):
         one_group(group, False)
 
-    out[...] = (total[...] * scale[...]).astype(jnp.bfloat16)
+    half = width // 2
+    crossed = total[1] * COSINE[3]
+    product = total[0] + jnp.concatenate([-crossed[:, half:], crossed[:, :half]], axis=1)
+    out[...] = (product * row_values[2]).astype(jnp.bfloat16)
     for kind, source in enumerate((points, chunks)):
         rest = source.at[pl.ds(0, count - 1)]
         pltpu.make_async_copy(rest, rest, sent.at[kind]).wait()
@@ -243,17 +259,21 @@
     landing = (2 * side, count // (2 * side))
     turn = node_count / 16.0 / (2.0 * math.pi)
     row_x, row_y = node_points(row_first + jnp.arange(rows, dtype=jnp.int32), node_count)
-    spread = lambda v: jnp.broadcast_to(v[:, None], (rows, 128))
+    scale = impedance_rows / math.sqrt(2.0 * math.pi)
+    row_values = (*gridded((row_x * turn, row_y * turn), 0.0), scale)
+    table = jnp.concatenate([v.reshape(-1, 128) for v in row_values], axis=0)
+    table = jnp.pad(table, ((0, 128 - table.shape[0]), (0, 0)))
     vmem = pl.BlockSpec(memory_space=pltpu.VMEM)
     return pl.pallas_call(
         functools.partial(sketch_kernel, sides, 3),
         out_shape=jax.ShapeDtypeStruct((rows, width), jnp.bfloat16),
-        in_specs=[vmem] * 5,
+        in_specs=[vmem] * 3,
         out_specs=vmem,
         scratch_shapes=[
             pltpu.VMEM((*landing, capacity, width), jnp.bfloat16),
             pltpu.VMEM((*landing, 1, 2 * capacity), jnp.float32),
-            pltpu.VMEM((rows, width), jnp.float32),
+            pltpu.VMEM((3, rows, 128), jnp.float32),
+            pltpu.VMEM((2, rows, width), jnp.float32),
             pltpu.SemaphoreType.DMA((2,)),
             pltpu.SemaphoreType.DMA((2, landing[0])),
         ],
@@ -263,8 +283,7 @@
     )(
         chunks,
         points,
-        *(spread(v) for v in gridded((row_x * turn, row_y * turn), 0.0)),
-        spread(impedance_rows / math.sqrt(2.0 * math.pi)),
+        table,
     )
 
 
@@ -299,31 +318,33 @@
     sublane = lax.broadcasted_iota(jnp.int32, (8, lanes), 0)
     twice = lambda v: jnp.concatenate([v, v], axis=1)
     done = []
-    for top in range(pieces):
+    for top in range(0, pieces, 2):
         columns = [
-            [
-                jnp.take_along_axis(
+            {
+                i: jnp.take_along_axis(
                     rows[i][:, :lanes],
                     jnp.full((8, lanes), first + 8 * top + t, jnp.int32),
                     axis=1,
                 )
                 for i in range(top, pieces)
-            ]
-            for t in range(8)
+            }
+            for t in range(16)
         ]
-        for t in range(8):
-            pivot = spread_rows(columns[t][0][t : t + 1], 8)
+        for t in range(16):
+            here, at = top + t // 8, t % 8
+            pivot = spread_rows(columns[t][here][at : at + 1], 8)
             inverse = 1.0 / pivot
-            row = rows[top][t : t + 1]
+            row = rows[here][at : at + 1]
             done.append(row * twice(lax.rsqrt(pivot[0:1])))
-            factors = [c * inverse for c in columns[t]]
-            factors[0] = jnp.where(sublane > t, factors[0], 0.0)
-            for u in range(t + 1, 8):
-                entry = spread_rows(columns[u][0][t : t + 1], 8)
-                columns[u] = [c - f * entry for c, f in zip(columns[u], factors)]
+            factors = {i: columns[t][i] * inverse for i in range(here, pieces)}
+            factors[here] = jnp.where(sublane > at, factors[here], 0.0)
+            for u in range(t + 1, 16):
+                entry = spread_rows(columns[u][here][at : at + 1], 8)
+                for i, f in factors.items():
+                    columns[u][i] = columns[u][i] - f * entry
             full_row = spread_rows(row, 8)
-            for i, f in enumerate(factors):
-                rows[top + i] = rows[top + i] - twice(f) * full_row
+            for i, f in factors.items():
+                rows[i] = rows[i] - twice(f) * full_row
     return jnp.concatenate(done, axis=0)
 
 

time: 115 us -> 113 us (0.983)
  Pallas kernels: 110 us -> 107 us
  local copies, waits for them, and re-layouts: 1.68 us -> 3.54 us
    unnamed x9, local copies, waits for them, and re-layouts: 0.9 us -> 3.54 us
    pallas_call x1, Pallas kernels: 33.3 us -> 31.1 us  [merged_bases(): pl.pallas_call(functools.partial(merge_kernel, rows), out_shape=jax.Shape...]
    pallas_call x1, Pallas kernels: 69.8 us -> 68.4 us  [sketch_rows(): pl.pallas_call(functools.partial(sketch_kernel, sides, 3), out_shape=jax....]
where the time goes in v4:
time: 113 us; the launch traced here: 111 us
  Pallas kernels  107 us (95%)
  local copies, waits for them, and re-layouts  3.54 us (3%)
    pallas_call x1, Pallas kernels, sketch_rows(): pl.pallas_call(functools.partial(sketch_kernel, sides, 3), out_shape=jax....  68.4 us
    pallas_call x1, Pallas kernels, merged_bases(): pl.pallas_call(functools.partial(merge_kernel, rows), out_shape=jax.Shape...  31.1 us
    pallas_call x1, Pallas kernels, packed_chunks(): pl.pallas_call(functools.partial(pack_kernel, capacity, node_count), out_...  7.04 us
    unnamed x9, local copies, waits for them, and re-layouts  3.54 us

profile of v4, /device:TPU:10, one launch (start us, length us, event | category | flops | bytes accessed | tf_op | source)
XLA Modules:
  0.0 111.0 jit_solution(17896424679880810560)
XLA Ops:
  0.0 0.0 copy-start.1
  0.0 0.7 multiply_bitcast_fusion
  0.7 0.1 multiply_multiply_fusion
  0.8 0.0 copy-start
  0.8 1.2 %copy-done = bf16[4096,128]{1,0:T(8,128)(2,1)S(1)} copy-done((bf16[4096,128]{1,0:T(8,128)(2,1)S(1)}, bf16[4096,128]{1,0:T(8,128)(2,1)}, u32[]{:S(2)}) %copy-start) | copy-done | bytes 1048600
  2.1 0.0 copy-start.2
  2.1 0.7 copy-done.2
  2.8 0.0 copy-start.3
  2.8 0.7 copy-done.3
  3.5 7.0 %shard_map.55 = (bf16[8192,128]{1,0:T(8,128)(2,1)S(1)}, f32[128,128]{1,0:T(8,128)S(1)}) custom-call(s32[32,128]{1,0:T(8,128)S(1)} %bitcast.12, s32[32,128]{1,0:T(8,128)S(1)} %bitcast.13, bf16[4096,128]{1,0:T(8,128)(2,1)S(1)} %copy-done), custom_call_target="tpu_custom_call" | custom-call | tf_op jit(solution)/shard_map/pallas_call | solution.py:98
  10.5 68.4 %shard_map.56.sketch = bf16[1536,128]{1,0:T(8,128)(2,1)S(1)} custom-call(bf16[128,64,128]{2,1,0:T(8,128)(2,1)S(1)} %bitcast.9, f32[128,1,128]{2,1,0:T(1,128)S(1)} %bitcast.11, f32[128,128]{1,0:T(8,128)S(1)} %select_maximum_fusion.row_table), custom_call_target="tpu_custom_call" | custom-call | tf_op jit(solution)/shard_map/pallas_call | solution.py:267
  78.9 0.0 copy-done.1
  78.9 31.1 %shard_map.57 = f32[1536,128]{1,0:T(8,128)S(1)} custom-call(bf16[1536,128]{1,0:T(8,128)(2,1)S(1)} %shard_map.56.sketch, bf16[4,128,128]{2,1,0:T(8,128)(2,1)S(1)} %bitcast.10), custom_call_target="tpu_custom_call" | custom-call | tf_op jit(solution)/shard_map/pallas_call | solution.py:451
  110.1 0.9 copy.7
  (1 shorter events, 0.0 us)
Async XLA Ops:
  0.0 78.9 %copy-start.1 = (bf16[1,4,128,128]{3,2,1,0:T(8,128)(2,1)S(1)}, bf16[1,4,128,128]{3,2,1,0:T(8,128)(2,1)}, u32[]{:S(2)}) copy-start(bf16[1,4,128,128]{3,2,1,0:T(8,128)(2,1)} %param.9) | copy-start | bytes 393220
  0.8 1.2 %copy-start = (bf16[4096,128]{1,0:T(8,128)(2,1)S(1)}, bf16[4096,128]{1,0:T(8,128)(2,1)}, u32[]{:S(2)}) copy-start(bf16[4096,128]{1,0:T(8,128)(2,1)} %omega.1) | copy-start | bytes 3145732
  2.1 0.7 copy-start.2
  2.8 0.7 copy-start.3

commit v5 on v4

--- a/solution.py
+++ b/solution.py
@@ -222,8 +222,7 @@
         weights = got[group].reshape(columns, width)
 
         if more:
-            @pl.loop(0, places)
-            def _(place):
+            for place in range(places):
                 send(group + lead, place)
         x, y = row_values[0], row_values[1]
         values = [kernel_values(x, y, a, b) for a, b in zip(col_x, col_y)]
@@ -435,11 +434,13 @@
     for batch in copies:
         for copy, _ in batch:
             copy.wait_send()
-    turned = split(turned, 1, (0, 1, 2))
-    sketch_here = sketch[...]
+    out[...] = split(turned, 1, (0, 1, 2))
+
+
+def bases_kernel(sketch, turned, out):
     out[...] = lax.dot_general(
-        jnp.concatenate([sketch_here] * 3, axis=1),
-        turned,
+        jnp.concatenate([sketch[...]] * 3, axis=1),
+        turned[...],
         (((1,), (1,)), ((), ())),
         preferred_element_type=jnp.float32,
     )
@@ -448,9 +449,9 @@
 def merged_bases(sketch, maps_here):
     rows, width = sketch.shape
     tile = (width, width)
-    return pl.pallas_call(
+    turned = pl.pallas_call(
         functools.partial(merge_kernel, rows),
-        out_shape=jax.ShapeDtypeStruct((rows, width), jnp.float32),
+        out_shape=jax.ShapeDtypeStruct((width, 3 * width), jnp.bfloat16),
         in_specs=[pl.BlockSpec(memory_space=pltpu.VMEM)] * 2,
         out_specs=pl.BlockSpec(memory_space=pltpu.VMEM),
         scratch_shapes=[
@@ -463,6 +464,15 @@
             collective_id=0, has_side_effects=True, vmem_limit_bytes=40 << 20
         ),
     )(sketch, maps_here)
+    row_spec = pl.BlockSpec((rows // 2, width), lambda i: (i, 0))
+    return pl.pallas_call(
+        bases_kernel,
+        grid=(2,),
+        out_shape=jax.ShapeDtypeStruct((rows, width), jnp.float32),
+        in_specs=[row_spec, pl.BlockSpec((width, 3 * width), lambda i: (0, 0))],
+        out_specs=row_spec,
+        compiler_params=pltpu.CompilerParams(vmem_limit_bytes=16 << 20),
+    )(sketch, turned)
 
 
 def sketch_of(omega, owners, columns, impedance):

time: 113 us -> 111 us (0.982)
  Pallas kernels: 107 us -> 105 us
    pallas_call x1, Pallas kernels: 68.4 us -> 65.8 us  [sketch_rows(): pl.pallas_call(functools.partial(sketch_kernel, sides, 3), out_shape=jax....]
    pallas_call x0 -> x1, Pallas kernels: none -> 1.4 us  [merged_bases(): pl.pallas_call(bases_kernel, grid=(2,), out_shape=jax.ShapeDtypeStruct((r...]
    unnamed x9 -> x8, local copies, waits for them, and re-layouts: 3.54 us -> 2.66 us
where the time goes in v5:
time: 111 us; the launch traced here: 108 us
  Pallas kernels  105 us (95%)
  local copies, waits for them, and re-layouts  2.66 us (2%)
    pallas_call x1, Pallas kernels, sketch_rows(): pl.pallas_call(functools.partial(sketch_kernel, sides, 3), out_shape=jax....  65.8 us
    pallas_call x1, Pallas kernels, merged_bases(): pl.pallas_call(functools.partial(merge_kernel, rows), out_shape=jax.Shape...  30.7 us
    pallas_call x1, Pallas kernels, packed_chunks(): pl.pallas_call(functools.partial(pack_kernel, capacity, node_count), out_...  7.04 us
    unnamed x8, local copies, waits for them, and re-layouts  2.66 us

profile of v5, /device:TPU:10, one launch (start us, length us, event | category | flops | bytes accessed | tf_op | source)
XLA Modules:
  0.0 108.5 jit_solution(7548061112170395774)
XLA Ops:
  0.0 0.0 copy-start.1
  0.0 0.7 multiply_bitcast_fusion
  0.7 0.1 multiply_multiply_fusion
  0.8 0.0 copy-start
  0.8 1.2 %copy-done = bf16[4096,128]{1,0:T(8,128)(2,1)S(1)} copy-done((bf16[4096,128]{1,0:T(8,128)(2,1)S(1)}, bf16[4096,128]{1,0:T(8,128)(2,1)}, u32[]{:S(2)}) %copy-start) | copy-done | bytes 1048600
  2.1 0.0 copy-start.2
  2.1 0.7 copy-done.2
  2.8 0.0 copy-start.3
  2.8 0.7 copy-done.3
  3.5 7.0 %shard_map.55 = (bf16[8192,128]{1,0:T(8,128)(2,1)S(1)}, f32[128,128]{1,0:T(8,128)S(1)}) custom-call(s32[32,128]{1,0:T(8,128)S(1)} %bitcast.11, s32[32,128]{1,0:T(8,128)S(1)} %bitcast.12, bf16[4096,128]{1,0:T(8,128)(2,1)S(1)} %copy-done), custom_call_target="tpu_custom_call" | custom-call | tf_op jit(solution)/shard_map/pallas_call | solution.py:98
  10.5 65.8 %shard_map.56.sketch = bf16[1536,128]{1,0:T(8,128)(2,1)S(1)} custom-call(bf16[128,64,128]{2,1,0:T(8,128)(2,1)S(1)} %bitcast.8, f32[128,1,128]{2,1,0:T(1,128)S(1)} %bitcast.10, f32[128,128]{1,0:T(8,128)S(1)} %select_maximum_fusion.row_table), custom_call_target="tpu_custom_call" | custom-call | tf_op jit(solution)/shard_map/pallas_call | solution.py:266
  76.4 0.0 copy-done.1
  76.4 30.7 %shard_map.57.turned = bf16[128,384]{1,0:T(8,128)(2,1)S(1)} custom-call(bf16[1536,128]{1,0:T(8,128)(2,1)S(1)} %shard_map.56.sketch, bf16[4,128,128]{2,1,0:T(8,128)(2,1)S(1)} %bitcast.9), custom_call_target="tpu_custom_call" | custom-call | tf_op jit(solution)/shard_map/pallas_call | solution.py:452
  107.1 1.4 %shard_map.58 = f32[1536,128]{1,0:T(8,128)} custom-call(bf16[1536,128]{1,0:T(8,128)(2,1)S(1)} %shard_map.56.sketch, bf16[128,384]{1,0:T(8,128)(2,1)S(1)} %shard_map.57.turned), custom_call_target="tpu_custom_call" | custom-call | tf_op jit(solution)/shard_map/pallas_call | solution.py:468
  (1 shorter events, 0.0 us)
Async XLA Ops:
  0.0 76.4 %copy-start.1 = (bf16[1,4,128,128]{3,2,1,0:T(8,128)(2,1)S(1)}, bf16[1,4,128,128]{3,2,1,0:T(8,128)(2,1)}, u32[]{:S(2)}) copy-start(bf16[1,4,128,128]{3,2,1,0:T(8,128)(2,1)} %param.9) | copy-start | bytes 393220
  0.8 1.2 %copy-start = (bf16[4096,128]{1,0:T(8,128)(2,1)S(1)}, bf16[4096,128]{1,0:T(8,128)(2,1)}, u32[]{:S(2)}) copy-start(bf16[4096,128]{1,0:T(8,128)(2,1)} %omega.1) | copy-start | bytes 3145732
  2.1 0.7 copy-start.2
  2.8 0.7 copy-start.3

commit v6 on v5

--- a/solution.py
+++ b/solution.py
@@ -22,8 +22,7 @@
 def pack_kernel(
     capacity,
     node_count,
-    owners,
-    columns,
+    codes,
     omega,
     chunks_out,
     points_out,
@@ -34,7 +33,7 @@
     plain,
     sem,
 ):
-    blocks, lanes = owners.shape
+    blocks, lanes = codes.shape
     count = points_out.shape[0]
     owner_at = lax.broadcasted_iota(jnp.int32, (count, lanes), 0)
     before = (
@@ -49,7 +48,8 @@
 
     def one_block(index, running):
         here = pl.ds(index, 1)
-        owner, column = owners[here, :], columns[here, :]
+        code = codes[here, :]
+        owner, column = code >> 15, code & 32767
         named = owner_at == owner
         onehot = named.astype(jnp.float32).astype(jnp.bfloat16)
         counts = jnp.dot(onehot, counted, preferred_element_type=jnp.float32)
@@ -94,6 +94,7 @@
     lanes = 128
     blocks = samples // lanes
     capacity = 2 * samples // count
+    codes = owners.reshape(blocks, lanes) * 32768 + columns.reshape(blocks, lanes)
     vmem = pl.BlockSpec(memory_space=pltpu.VMEM)
     return pl.pallas_call(
         functools.partial(pack_kernel, capacity, node_count),
@@ -101,7 +102,7 @@
             jax.ShapeDtypeStruct((count * capacity, width), jnp.bfloat16),
             jax.ShapeDtypeStruct((count, 2 * capacity), jnp.float32),
         ),
-        in_specs=[vmem] * 3,
+        in_specs=[vmem] * 2,
         out_specs=(vmem, vmem),
         scratch_shapes=[
             pltpu.VMEM((blocks, lanes), jnp.int32),
@@ -112,7 +113,7 @@
             pltpu.SemaphoreType.DMA,
         ],
         compiler_params=pltpu.CompilerParams(vmem_limit_bytes=40 << 20),
-    )(owners.reshape(blocks, lanes), columns.reshape(blocks, lanes), omega)
+    )(codes, omega)
 
 
 def gridded(points, shift):

time: 111 us -> 111 us (level)
  other arithmetic: 0.83 us -> 2.29 us
  local copies, waits for them, and re-layouts: 2.66 us -> 1.22 us
    unnamed x8 -> x4, local copies, waits for them, and re-layouts: 2.66 us -> 1.22 us
where the time goes in v6:
time: 111 us; the launch traced here: 109 us
  Pallas kernels  105 us (95%)
  other arithmetic  2.29 us (2%)
  local copies, waits for them, and re-layouts  1.22 us (1%)
    pallas_call x1, Pallas kernels, sketch_rows(): pl.pallas_call(functools.partial(sketch_kernel, sides, 3), out_shape=jax....  65.8 us
    pallas_call x1, Pallas kernels, merged_bases(): pl.pallas_call(functools.partial(merge_kernel, rows), out_shape=jax.Shape...  30.7 us
    pallas_call x1, Pallas kernels, packed_chunks(): pl.pallas_call(functools.partial(pack_kernel, capacity, node_count), out_...  7.05 us

profile of v6, /device:TPU:10, one launch (start us, length us, event | category | flops | bytes accessed | tf_op | source)
XLA Modules:
  0.0 108.5 jit_solution(15227007973593970990)
XLA Ops:
  0.0 0.0 copy-start.1
  0.0 0.7 multiply_bitcast_fusion
  0.7 0.1 multiply_multiply_fusion
  0.8 0.7 broadcast_multiply_fusion
  1.6 0.7 bitcast_add_fusion.codes
  2.3 0.0 copy-start
  2.3 1.2 %copy-done = bf16[4096,128]{1,0:T(8,128)(2,1)S(1)} copy-done((bf16[4096,128]{1,0:T(8,128)(2,1)S(1)}, bf16[4096,128]{1,0:T(8,128)(2,1)}, u32[]{:S(2)}) %copy-start) | copy-done | bytes 1048600
  3.5 7.0 %shard_map.55 = (bf16[8192,128]{1,0:T(8,128)(2,1)S(1)}, f32[128,128]{1,0:T(8,128)S(1)}) custom-call(s32[32,128]{1,0:T(8,128)S(1)} %bitcast_add_fusion.codes, bf16[4096,128]{1,0:T(8,128)(2,1)S(1)} %copy-done), custom_call_target="tpu_custom_call" | custom-call | tf_op jit(solution)/shard_map/pallas_call | solution.py:99
  10.6 65.8 %shard_map.56.sketch = bf16[1536,128]{1,0:T(8,128)(2,1)S(1)} custom-call(bf16[128,64,128]{2,1,0:T(8,128)(2,1)S(1)} %bitcast.9, f32[128,1,128]{2,1,0:T(1,128)S(1)} %bitcast.11, f32[128,128]{1,0:T(8,128)S(1)} %select_maximum_fusion.row_table), custom_call_target="tpu_custom_call" | custom-call | tf_op jit(solution)/shard_map/pallas_call | solution.py:267
  76.4 0.0 copy-done.1
  76.4 30.7 %shard_map.57.turned = bf16[128,384]{1,0:T(8,128)(2,1)S(1)} custom-call(bf16[1536,128]{1,0:T(8,128)(2,1)S(1)} %shard_map.56.sketch, bf16[4,128,128]{2,1,0:T(8,128)(2,1)S(1)} %bitcast.10), custom_call_target="tpu_custom_call" | custom-call | tf_op jit(solution)/shard_map/pallas_call | solution.py:453
  107.1 1.4 %shard_map.58 = f32[1536,128]{1,0:T(8,128)} custom-call(bf16[1536,128]{1,0:T(8,128)(2,1)S(1)} %shard_map.56.sketch, bf16[128,384]{1,0:T(8,128)(2,1)S(1)} %shard_map.57.turned), custom_call_target="tpu_custom_call" | custom-call | tf_op jit(solution)/shard_map/pallas_call | solution.py:469
  (1 shorter events, 0.0 us)
Async XLA Ops:
  0.0 76.4 %copy-start.1 = (bf16[1,4,128,128]{3,2,1,0:T(8,128)(2,1)S(1)}, bf16[1,4,128,128]{3,2,1,0:T(8,128)(2,1)}, u32[]{:S(2)}) copy-start(bf16[1,4,128,128]{3,2,1,0:T(8,128)(2,1)} %param.9) | copy-start | bytes 393220
  2.3 1.2 %copy-start = (bf16[4096,128]{1,0:T(8,128)(2,1)S(1)}, bf16[4096,128]{1,0:T(8,128)(2,1)}, u32[]{:S(2)}) copy-start(bf16[4096,128]{1,0:T(8,128)(2,1)} %omega.1) | copy-start | bytes 3145732
